TPU v7x, 256 devices: a whole 4x4x8 slice. The times are simulated.
256 devices in a mesh: pair: 128 (over z, y, x), blk: 2 (over core).
Axes of the slice: x: 4, y: 4, z: 8, core: 2. Of those that a mesh axis runs over, the one named last changes fastest.
Arguments:
- amplitudes: float32 [128, 1024, 1024], P('pair', 'blk'), may hold values from -6 to 6
- domain_mask: int32 [128, 16, 16], P('pair', 'blk'), may hold values 0 or 1
- integrals: float32 [2, 1024, 1024], P(None, 'blk'), may hold values from -0.125 to 0.125
Outputs:
- residual: float32 [64, 1024, 1024], P(None, ('blk', 'pair'))
All inputs are finite; a program needn't handle non-finite values. No bound on the sum of `domain_mask` on one device may be relied on, other than what follows from the above.
Results may differ from a plain program's by a relative error of at most 0.00007.
Values sent between devices are 32-bit elements; how exact they have to be, the bound alone decides.
No kernel may reach another device: no remote copies, remote signals or barrier semaphores. Data moves between devices by JAX's collectives and lax.ppermute only.
A program may use at most 64 MiB of HBM per device.

v0:
```python
import jax
import jax.numpy as jnp
from jax import lax
from jax.sharding import PartitionSpec as P

TILE = 64
NK = 2


def on_device(amplitudes, domain_mask, integrals):
    pairs_here, a_here, width = amplitudes.shape
    tiles_a = domain_mask.shape[1]
    tiles_c = domain_mask.shape[2]
    expanded = domain_mask.astype(jnp.float32)[:, :, None, :, None]
    masked = (amplitudes.reshape(pairs_here, tiles_a, TILE, tiles_c, TILE) * expanded).reshape(
        pairs_here, a_here, width
    )
    received = lax.all_to_all(masked, "pair", split_axis=1, concat_axis=0, tiled=True)
    total_pairs = received.shape[0]
    a_rows = received.shape[1]
    occupied = total_pairs // NK
    count_rows = occupied * a_rows
    ordered = (
        received.reshape(occupied, NK, a_rows, width)
        .transpose(0, 2, 1, 3)
        .reshape(count_rows, NK, width)
    )
    columns = integrals.shape[2]
    result = jnp.einsum(
        "rkc,kcb->rb",
        ordered,
        lax.all_gather(integrals, "blk", axis=1, tiled=True),
        precision=lax.Precision.HIGHEST,
        preferred_element_type=jnp.float32,
    )
    return result.reshape(occupied, a_rows, columns)


def solution(mesh):
    return jax.shard_map(
        on_device,
        mesh=mesh,
        in_specs=(P("pair", "blk", None), P("pair", "blk", None), P(None, "blk", None)),
        out_specs=P(None, ("blk", "pair"), None),
        check_vma=False,
    )
```

profile of v0, /device:TPU:16, one launch (start us, length us, event | category | flops | bytes accessed | tf_op | source)
XLA Modules:
  0.0 115.1 jit_solution(15712019885021302118)
XLA Ops:
  6.5 0.0 copy-start
  6.5 0.0 all-gather.2.cloned.1.call-start
  6.5 0.7 all-gather.2.cloned.1.call-update
  7.3 0.0 copy-done
  7.3 2.3 %mul.16 = f32[8,64,16,64]{3,2,1,0:T(8,128)} broadcast(f32[8,16]{1,0:T(8,128)S(1)} %convert_bitcast_fusion), dimensions={0,2} | broadcast | bytes 2097664 | tf_op jit(solution)/shard_map/mul | solution.py:15
  9.6 3.5 %mul.17 = f32[1,512,1024]{2,1,0:T(8,128)S(1)} reshape(f32[8,64,16,64]{3,2,1,0:T(8,128)} %mul.16) | data formatting | bytes 4194304 | tf_op jit(solution)/shard_map/mul | solution.py:15
  13.1 2.0 %mul.18 = f32[1,512,1024]{2,1,0:T(8,128)S(1)} multiply(f32[1,512,1024]{2,1,0:T(8,128)} %param.3, f32[1,512,1024]{2,1,0:T(8,128)S(1)} %mul.17) | non-fusion elementwise | flops 524288 | bytes 6291456 | tf_op jit(solution)/shard_map/mul | solution.py:15
  15.1 2.2 %copy.12 = f32[1,512,1024]{2,0,1:T(1,128)S(1)} copy(f32[1,512,1024]{2,1,0:T(8,128)S(1)} %mul.18) | data formatting | bytes 4194304 | tf_op jit(solution)/shard_map/mul | solution.py:15
  17.2 66.4 %all_to_all.4 = f32[1,512,1024]{2,0,1:T(1,128)S(1)} all-to-all(f32[1,512,1024]{2,0,1:T(1,128)S(1)} %copy.12), channel_id=1, replica_groups=mesh['pair'=128,'blk'=2] {'pair'}, dimensions={1} | all-to-all | bytes 4194304 | tf_op jit(solution)/shard_map/all_to_all | solution.py:18
  83.6 6.9 %reduce = f32[512,1024]{1,0:T(8,128)} reduce(f32[1,512,1024]{2,0,1:T(1,128)S(1)} %all_to_all.4, f32[]{:T(128)} %constant.2), dimensions={0}, to_apply=%all_to_all.2.reduce_sub_computation | reduce | bytes 4194308 | tf_op jit(solution)/shard_map/all_to_all | solution.py:18
  90.5 1.9 %reshape.23 = f32[64,2,4,1024]{3,2,1,0:T(4,128)S(1)} reshape(f32[512,1024]{1,0:T(8,128)} %reduce) | data formatting | bytes 4194304 | tf_op jit(solution)/shard_map/reshape | solution.py:24
  92.4 3.3 %copy.23 = f32[64,4,2,1024]{3,2,1,0:T(2,128)} copy(f32[64,4,2,1024]{3,1,2,0:T(4,128)S(1)} %bitcast.20) | data formatting | bytes 4194304 | tf_op jit(solution)/shard_map/transpose | solution.py:25
  95.6 0.0 all-gather.2.cloned.1.call-done
  95.6 11.0 %fusion.3 = f32[64,4,1024]{2,0,1:T(8,128)S(1)} fusion(f32[2,1024,1024]{2,1,0:T(8,128)} %all-gather.2.cloned.1.call-done, f32[64,4,1024,2]{2,3,1,0:T(2,128)} %bitcast.21), kind=kOutput, calls=%fused_computation.4 | convolution fusion | flops 6442450944 | bytes 11534336 | tf_op jit(solution)/shard_map/rkc,kcb->rb/dot_general | solution.py:29
  106.6 1.6 %copy.15 = f32[64,4,1024]{2,1,0:T(4,128)} copy(f32[64,4,1024]{2,0,1:T(8,128)S(1)} %fusion.3) | data formatting | bytes 2097152 | tf_op jit(solution)/shard_map/rkc,kcb->rb/dot_general | solution.py:29
  (1 shorter events, 0.0 us)
Async XLA Ops:
  6.5 0.7 copy-start
  6.5 89.1 %all-gather.2.cloned.1.call-start = ((), (), s32[]{:S(2)}) async-start(), calls=%async_computation.1 | async-start | bytes 12582912 | tf_op jit(solution)/shard_map/all_gather | solution.py:32
Sparse Core Ops, SparseCore 0:
  9.2 27.9 all-gather.1
where the time goes:
time: 117 us; the launch traced here: 115 us
  blocking collectives  66.4 us (57%)
  local copies, waits for them, and re-layouts  14.7 us (13%)
  between operations  13.4 us (11%)
  matrix products  11 us (9%)
  other arithmetic  8.87 us (8%)
    all_to_all x1, blocking collectives, on_device(): lax.all_to_all(masked, 'pair', split_axis=1, concat_axis=0, tiled=True)  66.4 us
    dot_general x1, matrix products, on_device(): jnp.einsum('rkc,kcb->rb', ordered, lax.all_gather(integrals, 'blk', axis=...  11 us
    mul x3, local copies, waits for them, and re-layouts, on_device(): amplitudes.reshape(pairs_here, tiles_a, TILE, tiles_c, TILE) * expanded  7.94 us
    all_to_all x1, other arithmetic, on_device(): lax.all_to_all(masked, 'pair', split_axis=1, concat_axis=0, tiled=True)  6.88 us
    transpose x1, local copies, waits for them, and re-layouts, on_device(): ordered = received.reshape(occupied, NK, a_rows, width).transpose(0, 2, 1...  3.27 us
  transfers between devices with their start and end apart: 1, of which 0 were waited for; matrix products, arithmetic and copies ran while one was open for 19% of the time, Pallas kernels for 0%

commit v1 on v0

v1 whole, which is shorter than its diff:
```python
import functools
import jax
import jax.numpy as jnp
from jax import lax
from jax.experimental import pallas as pl
from jax.experimental.pallas import tpu as pltpu
from jax.sharding import PartitionSpec as P

TILE = 64
LANES = 128
X = 4
R = 4
PIECES = 4


def vmem():
    return pl.BlockSpec(memory_space=pltpu.VMEM)


def smem():
    return pl.BlockSpec(memory_space=pltpu.SMEM)


def hbm():
    return pl.BlockSpec(memory_space=pltpu.HBM)


def split(value):
    high = value.astype(jnp.bfloat16)
    low = (value - high.astype(jnp.float32)).astype(jnp.bfloat16)
    return high, low


def dot(a, b):
    return jnp.dot(a, b, preferred_element_type=jnp.float32)


def product(a_high, a_low, b_high, b_low):
    return dot(a_high, b_high) + (dot(a_high, b_low) + dot(a_low, b_high))


def prepare_kernel(where_ref, t_ref, mask_ref, send_ref, own_ref, held_ref, mask_held, sems):
    rows, width = t_ref.shape[1:]
    tiles_a, tiles_c = mask_ref.shape[1:]
    groups = rows // (X * R)
    tiles = width // LANES
    mask_copy = pltpu.make_async_copy(mask_ref.at[0], mask_held, sems.at[tiles])
    mask_copy.start()
    copies = []
    for t in range(tiles):
        copy = pltpu.make_async_copy(t_ref.at[0, :, pl.ds(t * LANES, LANES)], held_ref.at[t], sems.at[t])
        copy.start()
        copies.append(copy)
    per_tile = groups // tiles_a
    pick = (
        lax.broadcasted_iota(jnp.int32, (groups, tiles_a), 0) // per_tile
        == lax.broadcasted_iota(jnp.int32, (groups, tiles_a), 1)
    ).astype(jnp.float32)
    spread = (
        lax.broadcasted_iota(jnp.int32, (tiles_c, width), 1) // TILE
        == lax.broadcasted_iota(jnp.int32, (tiles_c, width), 0)
    ).astype(jnp.float32)
    mask_copy.wait()
    mask = dot(dot(pick, mask_held[...].astype(jnp.float32)), spread)
    outer = where_ref[0] == 1
    for t in range(tiles):
        copies[t].wait()
        cols = pl.ds(t * LANES, LANES)
        m = mask[:, t * LANES : (t + 1) * LANES]
        for h in range(2):
            x_outer, x_inner = (0, 1) if h == 0 else (3, 2)
            x_own = jnp.where(outer, x_outer, x_inner)
            x_send = jnp.where(outer, x_inner, x_outer)
            for r in range(R):
                at = pl.ds((r * 2 + h) * groups, groups)
                own_ref[at, cols] = held_ref[t, pl.ds(x_own * R + r, groups, X * R), :] * m
                send_ref[at, cols] = held_ref[t, pl.ds(x_send * R + r, groups, X * R), :] * m


def near_kernel(where_ref, own_ref, send_ref, w_ref, *refs):
    part_kernel(where_ref, own_ref, send_ref, w_ref, None, None, *refs)


def part_kernel(where_ref, own_ref, send_ref, w_ref, own_first, send_first, *refs):
    own_part, send_part, high_ref, low_ref, held_ref, sems = refs
    k, half, blk = where_ref[1], where_ref[2], where_ref[3]
    depth = w_ref.shape[1]
    piece = depth // PIECES

    def copies(which, of):
        return [
            pltpu.make_async_copy(
                w_ref.at[of, pl.ds(q * piece, piece)],
                held_ref.at[which, pl.ds(q * piece, piece)],
                sems.at[which, q],
            )
            for q in range(PIECES)
        ]

    mine = copies(0, k)
    for copy in mine:
        copy.start()

    @pl.when(blk == 0)
    def _():
        for copy in copies(1, 1 - k):
            copy.start()

    for copy in mine:
        copy.wait()
    cols = pl.ds(pl.multiple_of(half * depth, depth), depth)
    w_high, w_low = split(held_ref[0])

    def add(x_ref, first_ref, to_ref):
        x_high, x_low = split(x_ref[:, cols])
        term = product(x_high, x_low, w_high, w_low)
        to_ref[...] = term if first_ref is None else first_ref[...] + term

    @pl.when(blk == 1)
    def _():
        add(send_ref, send_first, send_part)

    add(own_ref, own_first, own_part)

    @pl.when(blk == 0)
    def _():
        for copy in copies(1, 1 - k):
            copy.wait()
        o_high, o_low = split(held_ref[1])
        high_ref[...] = o_high
        low_ref[...] = o_low


def place(out_ref, total):
    rows, width = total.shape
    groups = rows // (2 * R)
    tiles = width // LANES
    per = R * tiles
    for r in range(R):
        for h in range(2):
            row = (r * 2 + h) * groups
            for t in range(tiles):
                out_ref[pl.ds(h * per + t * R + r, groups, 2 * per), :] = total[
                    row : row + groups, t * LANES : (t + 1) * LANES
                ]


def last_kernel(where_ref, rows_ref, sums_ref, high0_ref, low0_ref, high1_ref, low1_ref, part_ref, out_ref):
    half, blk = where_ref[2], where_ref[3]
    depth = high0_ref.shape[0]

    @pl.when(blk == 0)
    def _():
        total = part_ref[...]
        for at, high, low in ((half, high0_ref, low0_ref), (1 - half, high1_ref, low1_ref)):
            cols = pl.ds(pl.multiple_of(at * depth, depth), depth)
            a_high, a_low = split(rows_ref[:, cols])
            total = total + product(a_high, a_low, high[...], low[...])
        place(out_ref, total)

    @pl.when(blk == 1)
    def _():
        place(out_ref, sums_ref[...] + part_ref[...])


def call(kernel, name, out_shape, in_specs, scratch=()):
    return pl.pallas_call(
        kernel,
        out_shape=out_shape,
        in_specs=in_specs,
        out_specs=jax.tree.map(lambda _: vmem(), out_shape),
        scratch_shapes=list(scratch),
        compiler_params=pltpu.CompilerParams(vmem_limit_bytes=32 * 2**20),
        cost_estimate=pl.CostEstimate(flops=1000, bytes_accessed=1000, transcendentals=0),
        name=name,
    )


def on_device(n_pair, halves, amplitudes, domain_mask, integrals):
    f32, bf16 = jnp.float32, jnp.bfloat16

    def of(*shape, dtype=f32):
        return jax.ShapeDtypeStruct(shape, dtype)

    rows, width = amplitudes.shape[1:]
    depth, columns = integrals.shape[1:]
    kept = rows // 2
    dests = kept // R
    tiles = columns // LANES
    x = lax.axis_index("pair") % X
    blk = lax.axis_index("blk")
    outer = ((x == 0) | (x == 3)).astype(jnp.int32)
    where = jnp.stack([outer, x % 2, blk, blk]).astype(jnp.int32)
    where_other = jnp.stack([outer, x % 2, 1 - blk, blk]).astype(jnp.int32)
    swaps = [[(2 * p + core, 2 * (p ^ 1) + core) for p in range(n_pair)] for core in range(2)]

    other = lax.ppermute(integrals, "blk", [(0, 1), (1, 0)])
    send, own = call(
        prepare_kernel,
        "prepare",
        [of(kept, width)] * 2,
        [smem(), hbm(), hbm()],
        [
            pltpu.VMEM((width // LANES, rows, LANES), f32),
            pltpu.VMEM(domain_mask.shape[1:], jnp.int32),
            pltpu.SemaphoreType.DMA((width // LANES + 1,)),
        ],
    )(where, amplitudes, domain_mask)
    got_rows = lax.ppermute(send, ("pair", "blk"), swaps[0])

    outs = [of(kept, columns)] * 2 + [of(depth, columns, dtype=bf16)] * 2
    scratch = [pltpu.VMEM((2, depth, columns), f32), pltpu.SemaphoreType.DMA((2, PIECES))]
    own_part, send_part, high0, low0 = call(
        near_kernel, "near", outs, [smem(), vmem(), vmem(), hbm()], scratch
    )(where, own, send, integrals)
    own_part, send_part, high1, low1 = call(
        part_kernel, "far", outs, [smem(), vmem(), vmem(), hbm(), vmem(), vmem()], scratch
    )(where_other, own, send, other, own_part, send_part)
    got_sums = lax.ppermute(send_part, ("pair", "blk"), swaps[1])
    block = call(last_kernel, "last", of(dests * R * tiles, LANES), [smem()] + [vmem()] * 7)(
        where, got_rows, got_sums, high0, low0, high1, low1, own_part
    )
    back = lax.all_to_all(
        block.reshape(dests, R * tiles, LANES),
        "pair",
        split_axis=0,
        concat_axis=0,
        tiled=True,
        axis_index_groups=halves,
    )
    return back.reshape(dests, tiles, R, LANES).transpose(0, 2, 1, 3).reshape(dests, R, columns)


def solution(mesh):
    n_pair = mesh.shape["pair"]
    halves = [
        [p for p in range(n_pair) if p % X in (0, 3)],
        [p for p in range(n_pair) if p % X in (1, 2)],
    ]
    return jax.shard_map(
        functools.partial(on_device, n_pair, halves),
        mesh=mesh,
        in_specs=(P("pair", "blk", None), P("pair", "blk", None), P(None, "blk", None)),
        out_specs=P(None, ("blk", "pair"), None),
        check_vma=False,
    )
```

time: 117 us -> 73.1 us (0.62)
  the two profiles are of different devices: /device:TPU:16 before, /device:TPU:1 now
where the time goes in v1:
time: 73.1 us; the launch traced here: 72.8 us
  blocking collectives  35.1 us (48%)
  waiting for transfers between devices  14.7 us (20%)
  Pallas kernels  11.2 us (15%)
  starting transfers between devices  5.89 us (8%)
  local copies, waits for them, and re-layouts  5.84 us (8%)
    all_to_all x1, blocking collectives, on_device(): lax.all_to_all(block.reshape(dests, R * tiles, LANES), 'pair', split_axis...  35.1 us
    ppermute x1, waiting for transfers between devices, on_device(): got_sums = lax.ppermute(send_part, ('pair', 'blk'), swaps[1])  14.7 us
    pallas_call x1, Pallas kernels, on_device(): call(part_kernel, 'far', outs, [smem(), vmem(), vmem(), hbm(), vmem(), vm...  4.53 us
    unnamed x6, local copies, waits for them, and re-layouts  4.46 us
    ppermute x1, starting transfers between devices, on_device(): other = lax.ppermute(integrals, 'blk', [(0, 1), (1, 0)])  3.24 us
    pallas_call x1, Pallas kernels, on_device(): call(near_kernel, 'near', outs, [smem(), vmem(), vmem(), hbm()], scratch)  3.16 us
    pallas_call x1, Pallas kernels, on_device(): call(prepare_kernel, 'prepare', [of(kept, width)] * 2, [smem(), hbm(), hb...  1.92 us
    ppermute x1, starting transfers between devices, on_device(): got_sums = lax.ppermute(send_part, ('pair', 'blk'), swaps[1])  1.92 us
  transfers between devices with their start and end apart: 3, of which 1 were waited for; matrix products, arithmetic and copies ran while one was open for 0% of the time, Pallas kernels for 13%

profile of v1, /device:TPU:1, one launch (start us, length us, event | category | flops | bytes accessed | tf_op | source)
XLA Modules:
  0.0 72.8 jit_solution(13366506978264268315)
XLA Ops:
  0.0 3.2 %collective-permute-start.1 = (f32[2,512,1024]{2,1,0:T(8,128)}, f32[2,512,1024]{2,1,0:T(8,128)}, u32[]{:S(2)}, u32[]{:S(2)}) collective-permute-start(f32[2,512,1024]{2,1,0:T(8,128)} %w_ref.1), channel_id=1, source_target_pairs={{0,1},{1,0},{2,3},{3,2},{4,5},{5,4},{6,7},{7,6},{8,9},{9,8},{10,11... | collective-permute-start | bytes 12582920 | tf_op jit(solution)/shard_map/ppermute | solution.py:197
  3.2 0.1 add_add_fusion
  3.3 0.0 copy-start.1
  3.3 1.6 %copy-done.1 = f32[1,512,1024]{2,1,0:T(8,128)S(1)} copy-done((f32[1,512,1024]{2,1,0:T(8,128)S(1)}, f32[1,512,1024]{2,1,0:T(8,128)}, u32[]{:S(2)}) %copy-start.1) | copy-done | bytes 2097176
  4.9 0.0 copy-start.2
  4.9 0.7 copy-done.2
  5.6 1.9 %prepare.1 = (f32[256,1024]{1,0:T(8,128)S(1)}, f32[256,1024]{1,0:T(8,128)S(1)}) custom-call(s32[4]{0:T(128)S(1)} %get-tuple-element.25.where_ref, f32[1,512,1024]{2,1,0:T(8,128)S(1)} %copy-done.1, s32[1,8,16]{2,1,0:T(8,128)S(1)} %copy-done.2), custom_call_target="tpu_custom_call" | custom-call | flops 1000 | bytes 1000 | tf_op jit(solution)/shard_map/prepare/pallas_call | solution.py:198
  7.5 0.7 collective-permute-start
  8.3 0.0 copy-start
  8.3 2.2 %copy-done = f32[2,512,1024]{2,1,0:T(8,128)S(1)} copy-done((f32[2,512,1024]{2,1,0:T(8,128)S(1)}, f32[2,512,1024]{2,1,0:T(8,128)}, u32[]{:S(2)}) %copy-start) | copy-done | bytes 4194328
  10.5 3.2 %near.1 = (f32[256,1024]{1,0:T(8,128)S(1)}, f32[256,1024]{1,0:T(8,128)S(1)}, bf16[512,1024]{1,0:T(8,128)(2,1)S(1)}, bf16[512,1024]{1,0:T(8,128)(2,1)S(1)}) custom-call(s32[4]{0:T(128)S(1)} %get-tuple-element.25.where_ref, f32[256,1024]{1,0:T(8,128)S(1)} %get-tuple-element.16.own_ref, f32[256,1024]{1,0:T(8,128)S(1)} %get-tuple-element.15.send_ref, ...), custom_call_target="tpu_custom_call" | custom-call | flops 1000 | bytes 1000 | tf_op jit(solution)/shard_map/near/pallas_call | solution.py:213
  13.6 0.0 collective-permute-done.1.w_ref
  13.6 4.5 %far.1 = (f32[256,1024]{1,0:T(8,128)S(1)}, f32[256,1024]{1,0:T(8,128)S(1)}, bf16[512,1024]{1,0:T(8,128)(2,1)S(1)}, bf16[512,1024]{1,0:T(8,128)(2,1)S(1)}) custom-call(s32[4]{0:T(128)S(1)} %get-tuple-element.26.where_ref, f32[256,1024]{1,0:T(8,128)S(1)} %get-tuple-element.16.own_ref, f32[256,1024]{1,0:T(8,128)S(1)} %get-tuple-element.15.send_ref, ...), custom_call_target="tpu_custom_call" | custom-call | flops 1000 | bytes 1000 | tf_op jit(solution)/shard_map/far/pallas_call | solution.py:216
  18.2 1.9 %collective-permute-start.2 = (f32[256,1024]{1,0:T(8,128)S(1)}, f32[256,1024]{1,0:T(8,128)S(1)}, u32[]{:S(2)}, u32[]{:S(2)}) collective-permute-start(f32[256,1024]{1,0:T(8,128)S(1)} %get-tuple-element.19), channel_id=1, source_target_pairs={{1,3},{3,1},{5,7},{7,5},{9,11},{11,9},{13,15},{15,13},{17,19},{19,... | collective-permute-start | bytes 3145736 | tf_op jit(solution)/shard_map/ppermute | solution.py:219
  20.1 0.0 collective-permute-done.rows_ref
  20.1 14.7 %collective-permute-done.2.sums_ref = f32[256,1024]{1,0:T(8,128)S(1)} collective-permute-done((f32[256,1024]{1,0:T(8,128)S(1)}, f32[256,1024]{1,0:T(8,128)S(1)}, u32[]{:S(2)}, u32[]{:S(2)}) %collective-permute-start.2) | collective-permute-done | bytes 1048608 | tf_op jit(solution)/shard_map/ppermute | solution.py:219
  34.8 1.5 %last.1 = f32[2048,128]{1,0:T(8,128)S(1)} custom-call(s32[4]{0:T(128)S(1)} %get-tuple-element.25.where_ref, f32[256,1024]{1,0:T(8,128)S(1)} %collective-permute-done.rows_ref, f32[256,1024]{1,0:T(8,128)S(1)} %collective-permute-done.2.sums_ref, bf16[512,1024]{1,0:T(8,128)(2,1)S(1)} %get-tuple-element.20.high0_ref, ...), custom_call_target="tpu_custom_call" | custom-call | flops 1000 | bytes 1000 | tf_op jit(solution)/shard_map/last/pallas_call | solution.py:220
  36.3 35.1 %all_to_all.5 = f32[64,32,128]{2,1,0:T(8,128)S(1)} all-to-all(f32[64,32,128]{2,1,0:T(8,128)S(1)} %bitcast.11), channel_id=1, replica_groups={{0,6,8,14,16,22,24,30,32,38,40,46,48,54,56,62,64,70,72,78,80,86,88,94,9..., dimensions={0} | all-to-all | bytes 2097152 | tf_op jit(solution)/shard_map/all_to_all | solution.py:223
  71.4 0.1 copy.6
  71.5 1.3 %reshape.11 = f32[64,4,1024]{2,1,0:T(4,128)} reshape(f32[64,4,8,128]{3,2,1,0:T(8,128)S(1)} %bitcast.13) | data formatting | bytes 2097152 | tf_op jit(solution)/shard_map/reshape | solution.py:231
Async XLA Ops:
  0.0 13.6 %collective-permute-start.1 = (f32[2,512,1024]{2,1,0:T(8,128)}, f32[2,512,1024]{2,1,0:T(8,128)}, u32[]{:S(2)}, u32[]{:S(2)}) collective-permute-start(f32[2,512,1024]{2,1,0:T(8,128)} %w_ref.1), channel_id=1, source_target_pairs={{0,1},{1,0},{2,3},{3,2},{4,5},{5,4},{6,7},{7,6},{8,9},{9,8},{10,11... | collective-permute-start | bytes 12582920 | tf_op jit(solution)/shard_map/ppermute | solution.py:197
  3.3 1.6 %copy-start.1 = (f32[1,512,1024]{2,1,0:T(8,128)S(1)}, f32[1,512,1024]{2,1,0:T(8,128)}, u32[]{:S(2)}) copy-start(f32[1,512,1024]{2,1,0:T(8,128)} %t_ref.1) | copy-start | bytes 6291460
  4.9 0.7 copy-start.2
  7.5 12.6 %collective-permute-start = (f32[256,1024]{1,0:T(8,128)S(1)}, f32[256,1024]{1,0:T(8,128)S(1)}, u32[]{:S(2)}, u32[]{:S(2)}) collective-permute-start(f32[256,1024]{1,0:T(8,128)S(1)} %get-tuple-element.15.send_ref), channel_id=1, source_target_pairs={{0,2},{2,0},{4,6},{6,4},{8,10},{10,8},{12,14},{14,12},{16,18},{18,... | collective-permute-start | bytes 3145736 | tf_op jit(solution)/shard_map/ppermute | solution.py:209
  8.3 2.2 %copy-start = (f32[2,512,1024]{2,1,0:T(8,128)S(1)}, f32[2,512,1024]{2,1,0:T(8,128)}, u32[]{:S(2)}) copy-start(f32[2,512,1024]{2,1,0:T(8,128)} %w_ref.1) | copy-start | bytes 12582916
  18.2 16.6 %collective-permute-start.2 = (f32[256,1024]{1,0:T(8,128)S(1)}, f32[256,1024]{1,0:T(8,128)S(1)}, u32[]{:S(2)}, u32[]{:S(2)}) collective-permute-start(f32[256,1024]{1,0:T(8,128)S(1)} %get-tuple-element.19), channel_id=1, source_target_pairs={{1,3},{3,1},{5,7},{7,5},{9,11},{11,9},{13,15},{15,13},{17,19},{19,... | collective-permute-start | bytes 3145736 | tf_op jit(solution)/shard_map/ppermute | solution.py:219

commit v2 on v0

v2 whole, which is shorter than its diff:
```python
import functools
import jax
import jax.numpy as jnp
from jax import lax
from jax.experimental import pallas as pl
from jax.experimental.pallas import tpu as pltpu
from jax.sharding import PartitionSpec as P

TILE = 64
LANES = 128
X = 4
Y = 4
Z = 8
R = 4
FIRST = (0, 2)
SECOND = (1, 3)
PIECES = 4
PIECE = 2 * R * Z
ADD_FLOPS = 10**11


def vmem():
    return pl.BlockSpec(memory_space=pltpu.VMEM)


def hbm():
    return pl.BlockSpec(memory_space=pltpu.HBM)


def in_hbm(value):
    return pltpu.with_memory_space_constraint(value, pltpu.HBM)


def here():
    me = lax.axis_index("pair")
    return lax.rem(me, X), lax.rem(lax.div(me, X), Y), lax.axis_index("blk")


def split(value):
    high = value.astype(jnp.bfloat16)
    low = (value - high.astype(jnp.float32)).astype(jnp.bfloat16)
    return high, low


def dot(a, b):
    return jnp.dot(a, b, preferred_element_type=jnp.float32)


def product(a_high, a_low, b_high, b_low):
    return dot(a_high, b_high) + (dot(a_high, b_low) + dot(a_low, b_high))


def tile_rows(mask_ref, shift, width):
    tiles = mask_ref.shape[1]
    column = lax.div(lax.broadcasted_iota(jnp.int32, (tiles, width), 1), TILE)
    spread = lax.rem(column + shift, tiles) == lax.broadcasted_iota(jnp.int32, (tiles, width), 0)
    return dot(mask_ref[...].astype(jnp.float32), spread.astype(jnp.float32))


def first_kernel(t_ref, mask_ref, near_ref, far_ref, held_ref, mask_held, sems):
    width = t_ref.shape[3]
    tiles = width // LANES
    x, y, blk = here()
    outer = (x == 0) | (x == X - 1)
    mask_copy = pltpu.make_async_copy(mask_ref.at[0], mask_held, sems.at[len(FIRST) * tiles])
    mask_copy.start()
    copies = []
    for t in range(tiles):
        lanes = pl.multiple_of(lax.rem(t + blk * (tiles // 2), tiles) * LANES, LANES)
        for j, dy in enumerate(FIRST):
            copy = pltpu.make_async_copy(
                t_ref.at[:, lax.rem(y + dy, Y), :, pl.ds(lanes, LANES)],
                held_ref.at[t, j],
                sems.at[t * len(FIRST) + j],
            )
            copy.start()
            copies.append(copy)
    mask_copy.wait()
    mask = tile_rows(mask_held, blk * (mask_ref.shape[2] // 2), width)
    for t in range(tiles):
        out_ref = near_ref if t < tiles // 2 else far_ref
        cols = pl.ds(t % (tiles // 2) * LANES, LANES)
        m = mask[:, t * LANES : (t + 1) * LANES]
        for j in range(len(FIRST)):
            copies[t * len(FIRST) + j].wait()
            rows = held_ref.at[t, j].reshape(Z * X * R, LANES)
            for r in range(R):
                for h in range(2):
                    x_outer, x_inner = (0, 1) if h == 0 else (3, 2)
                    a = rows[pl.ds(x_outer * R + r, Z, X * R), :]
                    b = rows[pl.ds(x_inner * R + r, Z, X * R), :]
                    out_ref[pl.ds(((j * R + r) * 2 + h) * Z, Z), cols] = jnp.where(outer, b, a) * m


def rest_kernel(t_ref, mask_ref, after_ref, rest_ref, held_ref, mask_held, sems):
    del after_ref
    rows, width = t_ref.shape[1:]
    part = rows // 4
    x, y, blk = here()
    outer = (x == 0) | (x == X - 1)
    plane = X * Y * R
    tiles = width // LANES
    mask_copy = pltpu.make_async_copy(mask_ref.at[0], mask_held, sems.at[tiles])
    mask_copy.start()
    copies = []
    for t in range(tiles):
        copy = pltpu.make_async_copy(t_ref.at[0, :, pl.ds(t * LANES, LANES)], held_ref.at[t], sems.at[t])
        copy.start()
        copies.append(copy)
    mask_copy.wait()
    mask = tile_rows(mask_held, 0, width)
    for t in range(tiles):
        copies[t].wait()
        cols = pl.ds(t * LANES, LANES)
        m = mask[:, t * LANES : (t + 1) * LANES]
        for c, chunk in enumerate((FIRST, SECOND)):
            for j, dy in enumerate(chunk):
                at_y = lax.rem(y + dy, Y) * (X * R)
                for r in range(R):
                    for h in range(2):
                        x_outer, x_inner = (0, 1) if h == 0 else (3, 2)
                        a = held_ref[t, pl.ds(at_y + (x_outer * R + r), Z, plane), :] * m
                        b = held_ref[t, pl.ds(at_y + (x_inner * R + r), Z, plane), :] * m
                        at = ((j * R + r) * 2 + h) * Z
                        rest_ref[pl.ds(c * part + at, Z), cols] = jnp.where(outer, a, b)
                        if c:
                            rest_ref[pl.ds(2 * part + at, Z), cols] = jnp.where(outer, b, a)


def own_kernel(has_first, x_ref, w_ref, *refs):
    x, _, blk = here()
    k = lax.rem(x, 2)
    half = 1 - blk if has_first else blk
    first_ref = refs[0] if has_first else None
    *part_refs, high_ref, low_ref, held_ref, sems = refs[has_first:]
    depth = w_ref.shape[1]
    piece = depth // PIECES
    copies = []
    for which, of in enumerate((k, 1 - k)):
        for q in range(PIECES):
            copy = pltpu.make_async_copy(
                w_ref.at[of, pl.ds(q * piece, piece)],
                held_ref.at[which, pl.ds(q * piece, piece)],
                sems.at[which, q],
            )
            copy.start()
            copies.append(copy)
    cols = pl.ds(pl.multiple_of(half * depth, depth), depth)
    x_high, x_low = split(x_ref[:, cols])
    total = first_ref[...] if has_first else None
    for copy in copies[:PIECES]:
        copy.wait()
    w_high, w_low = split(held_ref[0])
    term = product(x_high, x_low, w_high, w_low)
    total = term if total is None else total + term
    base = 0
    for part_ref in part_refs:
        count = part_ref.shape[0]
        part_ref[...] = total[base : base + count]
        base += count
    for copy in copies[PIECES:]:
        copy.wait()
    o_high, o_low = split(held_ref[1])
    high_ref[...] = o_high
    low_ref[...] = o_low


def near_kernel(got_ref, high_ref, low_ref, part_ref, out_ref):
    out_ref[...] = part_ref[...] + product(*split(got_ref[...]), high_ref[...], low_ref[...])


def last_kernel(got_ref, high_ref, low_ref, part_ref, out_ref):
    total = part_ref[...] + product(*split(got_ref[...]), high_ref[...], low_ref[...])
    n, tiles = len(FIRST), total.shape[1] // LANES
    for j in range(n):
        put(out_ref, total[j * PIECE : (j + 1) * PIECE], j * R * tiles, n * R * tiles)


def put(out_ref, total, start, block):
    tiles = total.shape[1] // LANES
    for r in range(R):
        for h in range(2):
            row = (r * 2 + h) * Z
            for t in range(tiles):
                out_ref[pl.ds(h * block + start + t * R + r, Z, 2 * block), :] = total[
                    row : row + Z, t * LANES : (t + 1) * LANES
                ]


def add_kernel(got_ref, part_ref, *out_refs):
    tiles = got_ref.shape[1] // LANES
    for j, out_ref in enumerate(out_refs):
        rows = pl.ds(j * PIECE, PIECE)
        put(out_ref, got_ref[rows, :] + part_ref[rows, :], 0, R * tiles)


def turn_kernel(in_ref, out_ref):
    block = out_ref.shape[0] // (2 * Z)
    for n in range(2 * Z):
        out_ref[pl.ds(n * block, block), :] = in_ref[pl.ds((n * len(FIRST) + 1) * block, block), :]


def gather_kernel(*refs):
    *in_refs, out_ref = refs
    block = in_refs[0].shape[0] // (2 * Z)
    for j, in_ref in enumerate(in_refs):
        for n in range(2 * Z):
            out_ref[pl.ds((n * len(in_refs) + j) * block, block), :] = in_ref[pl.ds(n * block, block), :]


def merge_kernel(first_ref, moved_ref, second_ref, out_ref):
    block = out_ref.shape[0] // (2 * Y * Z)
    _, here_y, _ = here()
    for dy in range(Y):
        y = lax.rem(here_y - dy + Y, Y)
        for n in range(2 * Z):
            if dy == FIRST[1]:
                value = moved_ref[pl.ds(n * block, block), :]
            elif dy == FIRST[0]:
                value = first_ref[pl.ds(n * len(FIRST) * block, block), :]
            else:
                value = second_ref[pl.ds((n * len(SECOND) + SECOND.index(dy)) * block, block), :]
            z, h = n // 2, n % 2
            out_ref[pl.ds(pl.multiple_of(((z * Y + y) * 2 + h) * block, block), block), :] = value


def call(kernel, name, out_shape, in_specs, scratch=(), flops=1000):
    return pl.pallas_call(
        kernel,
        out_shape=out_shape,
        in_specs=in_specs,
        out_specs=jax.tree.map(lambda _: vmem(), out_shape),
        scratch_shapes=list(scratch),
        compiler_params=pltpu.CompilerParams(vmem_limit_bytes=24 * 2**20),
        cost_estimate=pl.CostEstimate(flops=flops, bytes_accessed=1000, transcendentals=0),
        name=name,
    )


def on_device(n_pair, groups, amplitudes, domain_mask, integrals):
    f32, bf16 = jnp.float32, jnp.bfloat16

    def of(*shape, dtype=f32):
        return jax.ShapeDtypeStruct(shape, dtype)

    rows, width = amplitudes.shape[1:]
    depth, columns = integrals.shape[1:]
    kept = rows // 2
    dests = kept // R
    tiles = columns // LANES
    swap = [(p, p ^ 1) for p in range(n_pair)]
    other = lax.ppermute(integrals, "blk", [(0, 1), (1, 0)])
    n_tiles = width // LANES
    mask_scratch = pltpu.VMEM(domain_mask.shape[1:], jnp.int32)
    send_near, send_far = call(
        first_kernel,
        "first",
        [of(2 * PIECE, width // 2)] * 2,
        [hbm(), hbm()],
        [
            pltpu.VMEM((n_tiles, len(FIRST), Z, X * R, LANES), f32),
            mask_scratch,
            pltpu.SemaphoreType.DMA((len(FIRST) * n_tiles + 1,)),
        ],
    )(in_hbm(amplitudes.reshape(Z, Y, X * R, width)), in_hbm(domain_mask))
    got_near = lax.ppermute(send_near, "pair", swap)
    got_far = lax.ppermute(send_far, "pair", swap)
    rest = call(
        rest_kernel,
        "rest",
        of(6 * PIECE, width),
        [hbm(), hbm(), pl.BlockSpec(memory_space=pl.ANY)],
        [pltpu.VMEM((n_tiles, rows, LANES), f32), mask_scratch, pltpu.SemaphoreType.DMA((n_tiles + 1,))],
    )(in_hbm(amplitudes), in_hbm(domain_mask), send_far)

    halves_w = [of(depth, columns, dtype=bf16)] * 2
    scratch = [pltpu.VMEM((2, depth, columns), f32), pltpu.SemaphoreType.DMA((2, PIECES))]
    part, high0, low0 = call(
        functools.partial(own_kernel, False),
        "own_near",
        [of(6 * PIECE, columns)] + halves_w,
        [vmem(), hbm()],
        scratch,
    )(rest, in_hbm(integrals))
    part0, part1, send1, high1, low1 = call(
        functools.partial(own_kernel, True),
        "own_far",
        [of(2 * PIECE, columns)] * 3 + halves_w,
        [vmem(), hbm(), vmem()],
        scratch,
    )(rest, other, part)
    send1, got_near, got_far = lax.optimization_barrier((send1, got_near, got_far))
    got1 = lax.ppermute(send1, "pair", swap)

    def along_y(value, dy):
        perm = []
        for p in range(n_pair):
            pz, py, px = p // (X * Y), p // X % Y, p % X
            perm.append((p, (pz * Y + (py + dy) % Y) * X + px))
        return lax.ppermute(value, "pair", perm)

    def across(block):
        out = lax.all_to_all(
            block.reshape(2 * Z, -1, LANES),
            "pair",
            split_axis=0,
            concat_axis=0,
            tiled=True,
            axis_index_groups=groups,
        )
        return out.reshape(-1, LANES)

    half, piece = of(2 * PIECE * tiles, LANES), of(PIECE * tiles, LANES)
    part0 = call(near_kernel, "near", of(2 * PIECE, columns), [vmem()] * 4)(got_near, high0, low0, part0)
    block0 = call(last_kernel, "last", half, [vmem()] * 4)(got_far, high1, low1, part0)
    back0 = across(block0)
    pieces = call(add_kernel, "add", [piece] * 2, [vmem()] * 2, (), ADD_FLOPS)(got1, part1)
    pieces = [along_y(value, dy) for value, dy in zip(pieces, SECOND)]
    block1 = call(gather_kernel, "gather", half, [vmem()] * 2)(*pieces)
    back1 = across(block1)
    moved = along_y(call(turn_kernel, "turn", piece, [vmem()])(back0), FIRST[1])
    whole = call(merge_kernel, "merge", of(4 * PIECE * tiles, LANES), [vmem()] * 3)(back0, moved, back1)
    return whole.reshape(dests, tiles, R, LANES).transpose(0, 2, 1, 3).reshape(dests, R, columns)


def solution(mesh):
    n_pair = mesh.shape["pair"]
    groups = [
        [(z * Y + y) * X + x for z in range(Z) for x in pair] for y in range(Y) for pair in ((0, 3), (1, 2))
    ]
    return jax.shard_map(
        functools.partial(on_device, n_pair, groups),
        mesh=mesh,
        in_specs=(P("pair", "blk", None), P("pair", "blk", None), P(None, "blk", None)),
        out_specs=P(None, ("blk", "pair"), None),
        check_vma=False,
    )
```

time: 117 us -> 70.4 us (0.60); the launches traced: 115 us -> 70 us
  blocking collectives: 66.4 us -> 0 us
  waiting for transfers between devices: 0.71 us -> 36.4 us
  starting transfers between devices: 0.01 us -> 19.8 us
  local copies, waits for them, and re-layouts: 14.7 us -> 0 us
  Pallas kernels: 0 us -> 13.7 us
  between operations: 13.4 us -> 0.1 us
  matrix products: 11 us -> 0 us
  other arithmetic: 8.87 us -> 0 us
    all_to_all x1 -> x0, blocking collectives: 66.4 us -> none  [on_device(): lax.all_to_all(masked, 'pair', split_axis=1, concat_axis=0, tiled=True)]
    ppermute x0 -> x7, waiting for transfers between devices: none -> 18.8 us  [the longest x3 14.5 us: along_y(): return lax.ppermute(value, 'pair', perm)]
    all_to_all x0 -> x2, waiting for transfers between devices: none -> 17.5 us  [across(): lax.all_to_all(block.reshape(2 * Z, -1, LANES), 'pair', split_axis=0, con...]
    pallas_call x0 -> x10, Pallas kernels: none -> 13.7 us  [the longest x1 3.29 us: on_device(): call(functools.partial(own_kernel, False), 'own_near', [of(6 * PIECE, col...]
    all_to_all x0 -> x2, starting transfers between devices: none -> 13.7 us  [across(): lax.all_to_all(block.reshape(2 * Z, -1, LANES), 'pair', split_axis=0, con...]
    dot_general x1 -> x0, matrix products: 11 us -> none  [on_device(): jnp.einsum('rkc,kcb->rb', ordered, lax.all_gather(integrals, 'blk', axis=...]
    mul x3 -> x0, local copies, waits for them, and re-layouts: 7.94 us -> none  [on_device(): amplitudes.reshape(pairs_here, tiles_a, TILE, tiles_c, TILE) * expanded]
    all_to_all x1 -> x0, other arithmetic: 6.88 us -> none  [on_device(): lax.all_to_all(masked, 'pair', split_axis=1, concat_axis=0, tiled=True)]
  transfers between devices with their start and end apart: 1 -> 9, of which waited for: 0 -> 6; matrix products, arithmetic and copies ran while one was open for 19% -> 0% of each run, Pallas kernels for 0% -> 18%
where the time goes in v2:
time: 70.4 us; the launch traced here: 70 us
  waiting for transfers between devices  36.4 us (52%)
  starting transfers between devices  19.8 us (28%)
  Pallas kernels  13.7 us (19%)
    all_to_all x2, waiting for transfers between devices, across(): lax.all_to_all(block.reshape(2 * Z, -1, LANES), 'pair', split_axis=0, con...  17.5 us
    ppermute x3, waiting for transfers between devices, along_y(): return lax.ppermute(value, 'pair', perm)  14.5 us
    all_to_all x2, starting transfers between devices, across(): lax.all_to_all(block.reshape(2 * Z, -1, LANES), 'pair', split_axis=0, con...  13.7 us
    ppermute x1, waiting for transfers between devices, on_device(): got_far = lax.ppermute(send_far, 'pair', swap)  4.39 us
    pallas_call x1, Pallas kernels, on_device(): call(functools.partial(own_kernel, False), 'own_near', [of(6 * PIECE, col...  3.29 us
    ppermute x3, starting transfers between devices, along_y(): return lax.ppermute(value, 'pair', perm)  2.53 us
    pallas_call x1, Pallas kernels, on_device(): call(functools.partial(own_kernel, True), 'own_far', [of(2 * PIECE, colum...  2.33 us
    pallas_call x1, Pallas kernels, on_device(): call(rest_kernel, 'rest', of(6 * PIECE, width), [hbm(), hbm(), pl.BlockSp...  2.25 us
  transfers between devices with their start and end apart: 9, of which 6 were waited for; matrix products, arithmetic and copies ran while one was open for 0% of the time, Pallas kernels for 18%

profile of v2, /device:TPU:16, one launch (start us, length us, event | category | flops | bytes accessed | tf_op | source)
XLA Modules:
  0.0 70.0 jit_solution(14897352491178438244)
XLA Ops:
  0.0 0.0 collective-permute-start
  0.0 1.5 %first.1 = (f32[128,512]{1,0:T(8,128)S(1)}, f32[128,512]{1,0:T(8,128)S(1)}) custom-call(f32[8,4,16,1024]{3,2,1,0:T(8,128)} %bitcast.13, s32[1,8,16]{2,1,0:T(8,128)} %mask_ref.3), custom_call_target="tpu_custom_call" | custom-call | flops 1000 | bytes 1000 | tf_op jit(solution)/shard_map/first/pallas_call | solution.py:255
  1.5 1.6 %collective-permute-start.1 = (f32[128,512]{1,0:T(8,128)S(1)}, f32[128,512]{1,0:T(8,128)S(1)}, u32[]{:S(2)}, u32[]{:S(2)}) collective-permute-start(f32[128,512]{1,0:T(8,128)S(1)} %get-tuple-element.23), channel_id=1, source_target_pairs={{0,2},{2,0},{4,6},{6,4},{8,10},{10,8},{12,14},{14,12},{16,18},{18,... | collective-permute-start | bytes 786440 | tf_op jit(solution)/shard_map/ppermute | solution.py:266
  3.0 0.5 collective-permute-start.2
  3.6 2.2 %rest.1.x_ref = f32[384,1024]{1,0:T(8,128)S(1)} custom-call(f32[1,512,1024]{2,1,0:T(8,128)} %t_ref.1, s32[1,8,16]{2,1,0:T(8,128)} %mask_ref.3, f32[128,512]{1,0:T(8,128)S(1)} %get-tuple-element.20.after_ref), custom_call_target="tpu_custom_call" | custom-call | flops 1000 | bytes 1000 | tf_op jit(solution)/shard_map/rest/pallas_call | solution.py:268
  5.8 3.3 %own_near.1 = (f32[384,1024]{1,0:T(8,128)S(1)}, bf16[512,1024]{1,0:T(8,128)(2,1)S(1)}, bf16[512,1024]{1,0:T(8,128)(2,1)S(1)}) custom-call(f32[384,1024]{1,0:T(8,128)S(1)} %rest.1.x_ref, f32[2,512,1024]{2,1,0:T(8,128)} %w_ref.1), custom_call_target="tpu_custom_call" | custom-call | flops 1000 | bytes 1000 | tf_op jit(solution)/shard_map/own_near/pallas_call | solution.py:278
  9.1 0.0 collective-permute-done.w_ref
  9.2 2.3 %own_far.1 = (f32[128,1024]{1,0:T(8,128)S(1)}, f32[128,1024]{1,0:T(8,128)S(1)}, f32[128,1024]{1,0:T(8,128)S(1)}, bf16[512,1024]{1,0:T(8,128)(2,1)S(1)}, bf16[512,1024]{1,0:T(8,128)(2,1)S(1)}) custom-call(f32[384,1024]{1,0:T(8,128)S(1)} %rest.1.x_ref, f32[2,512,1024]{2,1,0:T(8,128)S(1)} %collective-permute-done.w_ref, f32[384,1024]{1,0:T(8,128)S(1)} %get-tuple-element.21.refs_0_), custom_call_target="tpu_custom_call" | custom-call | flops 1000 | bytes 1000 | tf_op jit(solution)/shard_map/own_far/pallas_call | solution.py:285
  11.5 0.0 collective-permute-done.1.got_ref
  11.5 4.4 %collective-permute-done.2.got_ref = f32[128,512]{1,0:T(8,128)S(1)} collective-permute-done((f32[128,512]{1,0:T(8,128)S(1)}, f32[128,512]{1,0:T(8,128)S(1)}, u32[]{:S(2)}, u32[]{:S(2)}) %collective-permute-start.2) | collective-permute-done | bytes 262176 | tf_op jit(solution)/shard_map/ppermute | solution.py:267
  15.9 1.5 %collective-permute-start.4 = (f32[128,1024]{1,0:T(8,128)S(1)}, f32[128,1024]{1,0:T(8,128)S(1)}, u32[]{:S(2)}, u32[]{:S(2)}) collective-permute-start(f32[128,1024]{1,0:T(8,128)S(1)} %get-tuple-element.31), channel_id=1, source_target_pairs={{0,2},{2,0},{4,6},{6,4},{8,10},{10,8},{12,14},{14,12},{16,18},{18,... | collective-permute-start | bytes 1572872 | tf_op jit(solution)/shard_map/ppermute | solution.py:293
  17.4 0.6 near.1.part_ref
  18.0 1.6 %last.1 = f32[1024,128]{1,0:T(8,128)} custom-call(f32[128,512]{1,0:T(8,128)S(1)} %collective-permute-done.2.got_ref, bf16[512,1024]{1,0:T(8,128)(2,1)S(1)} %get-tuple-element.25.high_ref, bf16[512,1024]{1,0:T(8,128)(2,1)S(1)} %get-tuple-element.26.low_ref, f32[128,1024]{1,0:T(8,128)S(1)} %near.1.part_ref), custom_call_target="tpu_custom_call" | custom-call | flops 1000 | bytes 1000 | tf_op jit(solution)/shard_map/last/pallas_call | solution.py:315
  19.6 10.1 %all-to-all-start = ((f32[16,64,128]{2,1,0:T(8,128)}), f32[16,64,128]{2,1,0:T(8,128)S(1)}, u32[]{:S(2)}, u32[]{:S(2)}) async-start(f32[16,64,128]{2,1,0:T(8,128)} %bitcast.1), calls=%async_computation | async-start | bytes 1048576 | tf_op jit(solution)/shard_map/all_to_all | solution.py:303
  29.7 0.0 collective-permute-done.4.got_ref
  29.7 0.3 add.1
  30.0 1.4 %collective-permute-start.5 = (f32[512,128]{1,0:T(8,128)S(1)}, f32[512,128]{1,0:T(8,128)S(1)}, u32[]{:S(2)}, u32[]{:S(2)}) collective-permute-start(f32[512,128]{1,0:T(8,128)S(1)} %get-tuple-element.33), channel_id=1, source_target_pairs={{0,8},{2,10},{4,12},{6,14},{8,16},{10,18},{12,20},{14,22},{16,24},... | collective-permute-start | bytes 786440 | tf_op jit(solution)/shard_map/ppermute | solution.py:300
  31.3 0.7 %collective-permute-start.6 = (f32[512,128]{1,0:T(8,128)S(1)}, f32[512,128]{1,0:T(8,128)S(1)}, u32[]{:S(2)}, u32[]{:S(2)}) collective-permute-start(f32[512,128]{1,0:T(8,128)S(1)} %get-tuple-element.34), channel_id=1, source_target_pairs={{0,24},{2,26},{4,28},{6,30},{8,0},{10,2},{12,4},{14,6},{16,8},{18,... | collective-permute-start | bytes 786440 | tf_op jit(solution)/shard_map/ppermute | solution.py:300
  32.1 5.3 %collective-permute-done.5.refs_0_ = f32[512,128]{1,0:T(8,128)S(1)} collective-permute-done((f32[512,128]{1,0:T(8,128)S(1)}, f32[512,128]{1,0:T(8,128)S(1)}, u32[]{:S(2)}, u32[]{:S(2)}) %collective-permute-start.5) | collective-permute-done | bytes 262176 | tf_op jit(solution)/shard_map/ppermute | solution.py:300
  37.4 1.0 %collective-permute-done.6.refs_1_ = f32[512,128]{1,0:T(8,128)S(1)} collective-permute-done((f32[512,128]{1,0:T(8,128)S(1)}, f32[512,128]{1,0:T(8,128)S(1)}, u32[]{:S(2)}, u32[]{:S(2)}) %collective-permute-start.6) | collective-permute-done | bytes 262176 | tf_op jit(solution)/shard_map/ppermute | solution.py:300
  38.4 0.8 %gather.1 = f32[1024,128]{1,0:T(8,128)} custom-call(f32[512,128]{1,0:T(8,128)S(1)} %collective-permute-done.5.refs_0_, f32[512,128]{1,0:T(8,128)S(1)} %collective-permute-done.6.refs_1_), custom_call_target="tpu_custom_call" | custom-call | flops 1000 | bytes 1000 | tf_op jit(solution)/shard_map/gather/pallas_call | solution.py:319
  39.3 8.5 %all-to-all-done = f32[16,64,128]{2,1,0:T(8,128)S(1)} async-done(((f32[16,64,128]{2,1,0:T(8,128)}), f32[16,64,128]{2,1,0:T(8,128)S(1)}, u32[]{:S(2)}, u32[]{:S(2)}) %all-to-all-start) | async-done | bytes 524320 | tf_op jit(solution)/shard_map/all_to_all | solution.py:303
  47.7 3.6 %all-to-all-start.1 = ((f32[16,64,128]{2,1,0:T(8,128)}), f32[16,64,128]{2,1,0:T(8,128)S(1)}, u32[]{:S(2)}, u32[]{:S(2)}) async-start(f32[16,64,128]{2,1,0:T(8,128)} %bitcast.3), calls=%async_computation.1 | async-start | bytes 1048576 | tf_op jit(solution)/shard_map/all_to_all | solution.py:303
  51.3 0.4 collective-permute-start.3
  51.7 8.1 %collective-permute-done.3.moved_ref = f32[512,128]{1,0:T(8,128)S(1)} collective-permute-done((f32[512,128]{1,0:T(8,128)S(1)}, f32[512,128]{1,0:T(8,128)S(1)}, u32[]{:S(2)}, u32[]{:S(2)}) %collective-permute-start.3) | collective-permute-done | bytes 262176 | tf_op jit(solution)/shard_map/ppermute | solution.py:300
  59.9 9.1 %all-to-all-done.1 = f32[16,64,128]{2,1,0:T(8,128)S(1)} async-done(((f32[16,64,128]{2,1,0:T(8,128)}), f32[16,64,128]{2,1,0:T(8,128)S(1)}, u32[]{:S(2)}, u32[]{:S(2)}) %all-to-all-start.1) | async-done | bytes 524320 | tf_op jit(solution)/shard_map/all_to_all | solution.py:303
  68.9 1.1 %merge.1 = f32[2048,128]{1,0:T(8,128)} custom-call(f32[1024,128]{1,0:T(8,128)S(1)} %bitcast.11, f32[512,128]{1,0:T(8,128)S(1)} %collective-permute-done.3.moved_ref, f32[1024,128]{1,0:T(8,128)S(1)} %bitcast.12), custom_call_target="tpu_custom_call" | custom-call | flops 1000 | bytes 1000 | tf_op jit(solution)/shard_map/merge/pallas_call | solution.py:322
  (1 shorter events, 0.0 us)
Async XLA Ops:
  0.0 9.1 %collective-permute-start = (f32[2,512,1024]{2,1,0:T(8,128)}, f32[2,512,1024]{2,1,0:T(8,128)S(1)}, u32[]{:S(2)}, u32[]{:S(2)}) collective-permute-start(f32[2,512,1024]{2,1,0:T(8,128)} %w_ref.1), channel_id=1, source_target_pairs={{0,1},{1,0},{2,3},{3,2},{4,5},{5,4},{6,7},{7,6},{8,9},{9,8},{10,11... | collective-permute-start | bytes 12582920 | tf_op jit(solution)/shard_map/ppermute | solution.py:252
  1.5 10.0 %collective-permute-start.1 = (f32[128,512]{1,0:T(8,128)S(1)}, f32[128,512]{1,0:T(8,128)S(1)}, u32[]{:S(2)}, u32[]{:S(2)}) collective-permute-start(f32[128,512]{1,0:T(8,128)S(1)} %get-tuple-element.23), channel_id=1, source_target_pairs={{0,2},{2,0},{4,6},{6,4},{8,10},{10,8},{12,14},{14,12},{16,18},{18,... | collective-permute-start | bytes 786440 | tf_op jit(solution)/shard_map/ppermute | solution.py:266
  3.0 12.8 %collective-permute-start.2 = (f32[128,512]{1,0:T(8,128)S(1)}, f32[128,512]{1,0:T(8,128)S(1)}, u32[]{:S(2)}, u32[]{:S(2)}) collective-permute-start(f32[128,512]{1,0:T(8,128)S(1)} %get-tuple-element.20.after_ref), channel_id=1, source_target_pairs={{0,2},{2,0},{4,6},{6,4},{8,10},{10,8},{12,14},{14,12},{16,18},{18,... | collective-permute-start | bytes 786440 | tf_op jit(solution)/shard_map/ppermute | solution.py:267
  15.9 13.8 %collective-permute-start.4 = (f32[128,1024]{1,0:T(8,128)S(1)}, f32[128,1024]{1,0:T(8,128)S(1)}, u32[]{:S(2)}, u32[]{:S(2)}) collective-permute-start(f32[128,1024]{1,0:T(8,128)S(1)} %get-tuple-element.31), channel_id=1, source_target_pairs={{0,2},{2,0},{4,6},{6,4},{8,10},{10,8},{12,14},{14,12},{16,18},{18,... | collective-permute-start | bytes 1572872 | tf_op jit(solution)/shard_map/ppermute | solution.py:293
  19.6 28.2 %all-to-all-start = ((f32[16,64,128]{2,1,0:T(8,128)}), f32[16,64,128]{2,1,0:T(8,128)S(1)}, u32[]{:S(2)}, u32[]{:S(2)}) async-start(f32[16,64,128]{2,1,0:T(8,128)} %bitcast.1), calls=%async_computation | async-start | bytes 1048576 | tf_op jit(solution)/shard_map/all_to_all | solution.py:303
  30.0 7.4 %collective-permute-start.5 = (f32[512,128]{1,0:T(8,128)S(1)}, f32[512,128]{1,0:T(8,128)S(1)}, u32[]{:S(2)}, u32[]{:S(2)}) collective-permute-start(f32[512,128]{1,0:T(8,128)S(1)} %get-tuple-element.33), channel_id=1, source_target_pairs={{0,8},{2,10},{4,12},{6,14},{8,16},{10,18},{12,20},{14,22},{16,24},... | collective-permute-start | bytes 786440 | tf_op jit(solution)/shard_map/ppermute | solution.py:300
  31.3 7.1 %collective-permute-start.6 = (f32[512,128]{1,0:T(8,128)S(1)}, f32[512,128]{1,0:T(8,128)S(1)}, u32[]{:S(2)}, u32[]{:S(2)}) collective-permute-start(f32[512,128]{1,0:T(8,128)S(1)} %get-tuple-element.34), channel_id=1, source_target_pairs={{0,24},{2,26},{4,28},{6,30},{8,0},{10,2},{12,4},{14,6},{16,8},{18,... | collective-permute-start | bytes 786440 | tf_op jit(solution)/shard_map/ppermute | solution.py:300
  47.7 21.2 %all-to-all-start.1 = ((f32[16,64,128]{2,1,0:T(8,128)}), f32[16,64,128]{2,1,0:T(8,128)S(1)}, u32[]{:S(2)}, u32[]{:S(2)}) async-start(f32[16,64,128]{2,1,0:T(8,128)} %bitcast.3), calls=%async_computation.1 | async-start | bytes 1048576 | tf_op jit(solution)/shard_map/all_to_all | solution.py:303
  51.3 8.5 %collective-permute-start.3 = (f32[512,128]{1,0:T(8,128)S(1)}, f32[512,128]{1,0:T(8,128)S(1)}, u32[]{:S(2)}, u32[]{:S(2)}) collective-permute-start(f32[512,128]{1,0:T(8,128)S(1)} %turn.1), channel_id=1, source_target_pairs={{0,16},{2,18},{4,20},{6,22},{8,24},{10,26},{12,28},{14,30},{16,0},... | collective-permute-start | bytes 786440 | tf_op jit(solution)/shard_map/ppermute | solution.py:300

commit v3 on v2

v3 whole, which is shorter than its diff:
```python
import functools
import jax
import jax.numpy as jnp
from jax import lax
from jax.experimental import pallas as pl
from jax.experimental.pallas import tpu as pltpu
from jax.sharding import PartitionSpec as P

TILE = 64
LANES = 128
X = 4
Y = 4
Z = 8
R = 4
FIRST = 2
MOVED = (1, 3)
SECOND = MOVED + (0,)
PARTS = 4
PIECE = 2 * R * Z
ADD_FLOPS = 10**11
START_Z = 5


def vmem():
    return pl.BlockSpec(memory_space=pltpu.VMEM)


def hbm():
    return pl.BlockSpec(memory_space=pltpu.HBM)


def in_hbm(value):
    return pltpu.with_memory_space_constraint(value, pltpu.HBM)


def here():
    me = lax.axis_index("pair")
    return lax.rem(me, X), lax.rem(lax.div(me, X), Y), lax.axis_index("blk")


def split(value):
    high = value.astype(jnp.bfloat16)
    low = (value - high.astype(jnp.float32)).astype(jnp.bfloat16)
    return high, low


def dot(a, b):
    return jnp.dot(a, b, preferred_element_type=jnp.float32)


def product(a_high, a_low, b_high, b_low):
    return dot(a_high, b_high) + (dot(a_high, b_low) + dot(a_low, b_high))


def tile_rows(mask_ref, shift, width):
    tiles = mask_ref.shape[1]
    column = lax.div(lax.broadcasted_iota(jnp.int32, (tiles, width), 1), TILE)
    spread = lax.rem(column + shift, tiles) == lax.broadcasted_iota(jnp.int32, (tiles, width), 0)
    return dot(mask_ref[...].astype(jnp.float32), spread.astype(jnp.float32))


def first_kernel(t_ref, mask_ref, out_ref, held_ref, mask_held, sems):
    width = t_ref.shape[3]
    tiles = width // LANES
    x, y, blk = here()
    partner = x + 1 - 2 * lax.rem(x, 2)
    mask_copy = pltpu.make_async_copy(mask_ref.at[0], mask_held, sems.at[tiles])
    mask_copy.start()
    copies = []
    for t in range(tiles):
        lanes = pl.multiple_of(lax.rem(t + blk * (tiles // 2), tiles) * LANES, LANES)
        copy = pltpu.make_async_copy(
            t_ref.at[:, lax.rem(y + FIRST, Y), :, pl.ds(lanes, LANES)], held_ref.at[t], sems.at[t]
        )
        copy.start()
        copies.append(copy)
    mask_copy.wait()
    mask = tile_rows(mask_held, blk * (mask_ref.shape[2] // 2), width)
    for t in range(tiles):
        cols = pl.ds(t * LANES, LANES)
        m = mask[:, t * LANES : (t + 1) * LANES]
        copies[t].wait()
        rows = held_ref.at[t].reshape(Z * X * R, LANES)
        for r in range(R):
            for h in range(2):
                value = rows[pl.ds(end(partner, h) * R + r, Z, X * R), :]
                out_ref[pl.ds((r * 2 + h) * Z, Z), cols] = value * m


def end(x, h):
    outer = (x == 0) | (x == X - 1)
    return jnp.where(outer, h * (X - 1), 1 + h)


def rest_kernel(t_ref, mask_ref, after_ref, rest_ref, held_ref, mask_held, sems):
    del after_ref
    rows, width = t_ref.shape[1:]
    x, y, blk = here()
    partner = x + 1 - 2 * lax.rem(x, 2)
    plane = X * Y * R
    tiles = width // LANES
    mask_copy = pltpu.make_async_copy(mask_ref.at[0], mask_held, sems.at[tiles])
    mask_copy.start()
    copies = []
    for t in range(tiles):
        copy = pltpu.make_async_copy(t_ref.at[0, :, pl.ds(t * LANES, LANES)], held_ref.at[t], sems.at[t])
        copy.start()
        copies.append(copy)
    mask_copy.wait()
    mask = tile_rows(mask_held, 0, width)
    wanted = [(dy, x) for dy in (FIRST,) + SECOND] + [(dy, partner) for dy in SECOND]
    for t in range(tiles):
        copies[t].wait()
        cols = pl.ds(t * LANES, LANES)
        m = mask[:, t * LANES : (t + 1) * LANES]
        for n, (dy, device) in enumerate(wanted):
            for h in range(2):
                base = (lax.rem(y + dy, Y) * X + end(device, h)) * R
                for r in range(R):
                    value = held_ref[t, pl.ds(base + r, Z, plane), :]
                    rest_ref[pl.ds(n * PIECE + (r * 2 + h) * Z, Z), cols] = value * m


def own_kernel(has_first, x_ref, w_ref, *refs):
    x, _, blk = here()
    k = lax.rem(x, 2)
    half = 1 - blk if has_first else blk
    first_ref = refs[0] if has_first else None
    *part_refs, high_ref, low_ref, held_ref, sems = refs[has_first:]
    depth = w_ref.shape[1]
    piece = depth // PARTS
    copies = []
    for which, of in enumerate((k, 1 - k)):
        for q in range(PARTS):
            copy = pltpu.make_async_copy(
                w_ref.at[of, pl.ds(q * piece, piece)],
                held_ref.at[which, pl.ds(q * piece, piece)],
                sems.at[which, q],
            )
            copy.start()
            copies.append(copy)
    cols = pl.ds(pl.multiple_of(half * depth, depth), depth)
    x_high, x_low = split(x_ref[:, cols])
    total = first_ref[...] if has_first else None
    for copy in copies[:PARTS]:
        copy.wait()
    w_high, w_low = split(held_ref[0])
    term = product(x_high, x_low, w_high, w_low)
    total = term if total is None else total + term
    base = 0
    for part_ref in part_refs:
        count = part_ref.shape[0]
        part_ref[...] = total[base : base + count]
        base += count
    for copy in copies[PARTS:]:
        copy.wait()
    o_high, o_low = split(held_ref[1])
    high_ref[...] = o_high
    low_ref[...] = o_low


def last_kernel(got_ref, high0_ref, low0_ref, high1_ref, low1_ref, part_ref, out_ref):
    depth = high0_ref.shape[0]
    total = part_ref[...]
    for n, (high_ref, low_ref) in enumerate(((high0_ref, low0_ref), (high1_ref, low1_ref))):
        total = total + product(*split(got_ref[:, n * depth : (n + 1) * depth]), high_ref[...], low_ref[...])
    put(out_ref, total)


def put(out_ref, total):
    tiles = total.shape[1] // LANES
    block = R * tiles
    for r in range(R):
        for h in range(2):
            row = (r * 2 + h) * Z
            for t in range(tiles):
                rows = total[row : row + Z, t * LANES : (t + 1) * LANES]
                out_ref[pl.ds(h * block + t * R + r, Z, 2 * block), :] = pltpu.roll(rows, Z - START_Z, 0)


def add_kernel(got_ref, part_ref, *out_refs):
    for n, out_ref in enumerate(out_refs):
        rows = pl.ds(n * PIECE, PIECE)
        put(out_ref, got_ref[rows, :] + part_ref[rows, :])


def gather_kernel(*refs):
    *in_refs, out_ref = refs
    block = in_refs[0].shape[0] // (2 * Z)
    for j, in_ref in enumerate(in_refs):
        for n in range(2 * Z):
            out_ref[pl.ds((n * len(in_refs) + j) * block, block), :] = in_ref[pl.ds(n * block, block), :]


def merge_kernel(moved_ref, second_ref, out_ref):
    block = out_ref.shape[0] // (2 * Y * Z)
    _, here_y, _ = here()
    for dy in range(Y):
        y = lax.rem(here_y - dy + Y, Y)
        for n in range(2 * Z):
            if dy == FIRST:
                value = moved_ref[pl.ds(n * block, block), :]
            else:
                value = second_ref[pl.ds((n * len(SECOND) + SECOND.index(dy)) * block, block), :]
            z, h = (n // 2 + START_Z) % Z, n % 2
            out_ref[pl.ds(pl.multiple_of(((z * Y + y) * 2 + h) * block, block), block), :] = value


def call(kernel, name, out_shape, in_specs, scratch=(), flops=1000):
    return pl.pallas_call(
        kernel,
        out_shape=out_shape,
        in_specs=in_specs,
        out_specs=jax.tree.map(lambda _: vmem(), out_shape),
        scratch_shapes=list(scratch),
        compiler_params=pltpu.CompilerParams(vmem_limit_bytes=24 * 2**20),
        cost_estimate=pl.CostEstimate(flops=flops, bytes_accessed=1000, transcendentals=0),
        name=name,
    )


def on_device(n_pair, groups, amplitudes, domain_mask, integrals):
    f32, bf16 = jnp.float32, jnp.bfloat16

    def of(*shape, dtype=f32):
        return jax.ShapeDtypeStruct(shape, dtype)

    rows, width = amplitudes.shape[1:]
    depth, columns = integrals.shape[1:]
    kept = rows // 2
    dests = kept // R
    tiles = columns // LANES
    swap = [(p, p ^ 1) for p in range(n_pair)]
    other = lax.ppermute(integrals, "blk", [(0, 1), (1, 0)])
    n_tiles = width // LANES
    mask_scratch = pltpu.VMEM(domain_mask.shape[1:], jnp.int32)
    send0 = call(
        first_kernel,
        "first",
        of(PIECE, width),
        [hbm(), hbm()],
        [
            pltpu.VMEM((n_tiles, Z, X * R, LANES), f32),
            mask_scratch,
            pltpu.SemaphoreType.DMA((n_tiles + 1,)),
        ],
    )(in_hbm(amplitudes.reshape(Z, Y, X * R, width)), in_hbm(domain_mask))
    got0 = lax.ppermute(send0, "pair", swap)
    rest = call(
        rest_kernel,
        "rest",
        of(7 * PIECE, width),
        [hbm(), hbm(), pl.BlockSpec(memory_space=pl.ANY)],
        [pltpu.VMEM((n_tiles, rows, LANES), f32), mask_scratch, pltpu.SemaphoreType.DMA((n_tiles + 1,))],
    )(in_hbm(amplitudes), in_hbm(domain_mask), send0)

    halves_w = [of(depth, columns, dtype=bf16)] * 2
    scratch = [pltpu.VMEM((2, depth, columns), f32), pltpu.SemaphoreType.DMA((2, PARTS))]
    part, high0, low0 = call(
        functools.partial(own_kernel, False),
        "own_near",
        [of(7 * PIECE, columns)] + halves_w,
        [vmem(), hbm()],
        scratch,
    )(rest, in_hbm(integrals))
    part0, *parts, high1, low1 = call(
        functools.partial(own_kernel, True),
        "own_far",
        [of(n * PIECE, columns) for n in (1, 2, 1, 2, 1)] + halves_w,
        [vmem(), hbm(), vmem()],
        scratch,
    )(rest, other, part)
    part_moved, part_own, send_moved, send_own = parts
    send_moved, send_own, _ = lax.optimization_barrier((send_moved, send_own, got0))
    got_moved = lax.ppermute(send_moved, "pair", swap)
    got_own = lax.ppermute(send_own, "pair", swap)

    def along_y(value, dy):
        perm = []
        for p in range(n_pair):
            pz, py, px = p // (X * Y), p // X % Y, p % X
            perm.append((p, (pz * Y + (py + dy) % Y) * X + px))
        return lax.ppermute(value, "pair", perm)

    def across(block):
        out = lax.all_to_all(
            block.reshape(2 * Z, -1, LANES),
            "pair",
            split_axis=0,
            concat_axis=0,
            tiled=True,
            axis_index_groups=groups,
        )
        return out.reshape(-1, LANES)

    piece = of(PIECE * tiles, LANES)
    back0 = across(call(last_kernel, "last", piece, [vmem()] * 6)(got0, high0, low0, high1, low1, part0))
    values = call(add_kernel, "add_moved", [piece] * 2, [vmem()] * 2)(got_moved, part_moved)
    pieces = [along_y(value, dy) for value, dy in zip(values, MOVED)]
    pieces += call(add_kernel, "add_own", [piece], [vmem()] * 2, (), ADD_FLOPS)(got_own, part_own)
    block1 = call(gather_kernel, "gather", of(len(SECOND) * PIECE * tiles, LANES), [vmem()] * len(pieces))(*pieces)
    back1 = across(block1)
    moved = along_y(back0, FIRST)
    whole = call(merge_kernel, "merge", of(dests * R * tiles, LANES), [vmem()] * 2)(moved, back1)
    return whole.reshape(dests, tiles, R, LANES).transpose(0, 2, 1, 3).reshape(dests, R, columns)


def solution(mesh):
    n_pair = mesh.shape["pair"]
    groups = [
        [((z + START_Z) % Z * Y + y) * X + x for z in range(Z) for x in pair] for y in range(Y) for pair in ((0, 3), (1, 2))
    ]
    return jax.shard_map(
        functools.partial(on_device, n_pair, groups),
        mesh=mesh,
        in_specs=(P("pair", "blk", None), P("pair", "blk", None), P(None, "blk", None)),
        out_specs=P(None, ("blk", "pair"), None),
        check_vma=False,
    )
```

time: 70.4 us -> 66.5 us (0.945)
  waiting for transfers between devices: 36.4 us -> 24 us
  starting transfers between devices: 19.8 us -> 27.8 us
    all_to_all x2, starting transfers between devices: 13.7 us -> 21.4 us  [across(): lax.all_to_all(block.reshape(2 * Z, -1, LANES), 'pair', split_axis=0, con...]
    all_to_all x2, waiting for transfers between devices: 17.5 us -> 10.6 us  [across(): lax.all_to_all(block.reshape(2 * Z, -1, LANES), 'pair', split_axis=0, con...]
    ppermute x3, waiting for transfers between devices: 14.5 us -> 11.2 us  [along_y(): return lax.ppermute(value, 'pair', perm)]
    ppermute x3, waiting for transfers between devices: 4.39 us -> 2.19 us  [the longest x1 2.18 us: on_device(): got_own = lax.ppermute(send_own, 'pair', swap)]
    pallas_call x10 -> x9, Pallas kernels: 13.7 us -> 13.8 us  [the longest x1 3.49 us: on_device(): call(functools.partial(own_kernel, False), 'own_near', [of(7 * PIECE, col...]
  transfers between devices with their start and end apart: 9 -> 9, of which waited for: 6 -> 5; matrix products, arithmetic and copies ran while one was open for 0% -> 0% of each run, Pallas kernels for 18% -> 19%
where the time goes in v3:
time: 66.5 us; the launch traced here: 65.7 us
  starting transfers between devices  27.8 us (42%)
  waiting for transfers between devices  24 us (36%)
  Pallas kernels  13.8 us (21%)
    all_to_all x2, starting transfers between devices, across(): lax.all_to_all(block.reshape(2 * Z, -1, LANES), 'pair', split_axis=0, con...  21.4 us
    ppermute x3, waiting for transfers between devices, along_y(): return lax.ppermute(value, 'pair', perm)  11.2 us
    all_to_all x2, waiting for transfers between devices, across(): lax.all_to_all(block.reshape(2 * Z, -1, LANES), 'pair', split_axis=0, con...  10.6 us
    pallas_call x1, Pallas kernels, on_device(): call(functools.partial(own_kernel, False), 'own_near', [of(7 * PIECE, col...  3.49 us
    ppermute x3, starting transfers between devices, along_y(): return lax.ppermute(value, 'pair', perm)  2.73 us
    pallas_call x1, Pallas kernels, on_device(): call(functools.partial(own_kernel, True), 'own_far', [of(n * PIECE, colum...  2.56 us
    ppermute x1, waiting for transfers between devices, on_device(): got_own = lax.ppermute(send_own, 'pair', swap)  2.18 us
    pallas_call x1, Pallas kernels, on_device(): call(rest_kernel, 'rest', of(7 * PIECE, width), [hbm(), hbm(), pl.BlockSp...  2.16 us
  transfers between devices with their start and end apart: 9, of which 5 were waited for; matrix products, arithmetic and copies ran while one was open for 0% of the time, Pallas kernels for 19%

profile of v3, /device:TPU:16, one launch (start us, length us, event | category | flops | bytes accessed | tf_op | source)
XLA Modules:
  0.0 65.7 jit_solution(15618172054591828212)
XLA Ops:
  0.0 0.0 collective-permute-start.1
  0.0 1.2 %first.1.after_ref = f32[64,1024]{1,0:T(8,128)S(1)} custom-call(f32[8,4,16,1024]{3,2,1,0:T(8,128)} %bitcast.11, s32[1,8,16]{2,1,0:T(8,128)} %mask_ref.3), custom_call_target="tpu_custom_call" | custom-call | flops 1000 | bytes 1000 | tf_op jit(solution)/shard_map/first/pallas_call | solution.py:237
  1.2 1.6 %collective-permute-start = (f32[64,1024]{1,0:T(8,128)S(1)}, f32[64,1024]{1,0:T(8,128)S(1)}, u32[]{:S(2)}, u32[]{:S(2)}) collective-permute-start(f32[64,1024]{1,0:T(8,128)S(1)} %first.1.after_ref), channel_id=1, source_target_pairs={{0,2},{2,0},{4,6},{6,4},{8,10},{10,8},{12,14},{14,12},{16,18},{18,... | collective-permute-start | bytes 786440 | tf_op jit(solution)/shard_map/ppermute | solution.py:248
  2.8 2.2 %rest.1.x_ref = f32[448,1024]{1,0:T(8,128)S(1)} custom-call(f32[1,512,1024]{2,1,0:T(8,128)} %t_ref.1, s32[1,8,16]{2,1,0:T(8,128)} %mask_ref.3, f32[64,1024]{1,0:T(8,128)S(1)} %first.1.after_ref), custom_call_target="tpu_custom_call" | custom-call | flops 1000 | bytes 1000 | tf_op jit(solution)/shard_map/rest/pallas_call | solution.py:249
  4.9 3.5 %own_near.1 = (f32[448,1024]{1,0:T(8,128)S(1)}, bf16[512,1024]{1,0:T(8,128)(2,1)S(1)}, bf16[512,1024]{1,0:T(8,128)(2,1)S(1)}) custom-call(f32[448,1024]{1,0:T(8,128)S(1)} %rest.1.x_ref, f32[2,512,1024]{2,1,0:T(8,128)} %w_ref.1), custom_call_target="tpu_custom_call" | custom-call | flops 1000 | bytes 1000 | tf_op jit(solution)/shard_map/own_near/pallas_call | solution.py:259
  8.4 0.0 collective-permute-done.1.w_ref
  8.4 2.6 %own_far.1 = (f32[64,1024]{1,0:T(8,128)S(1)}, f32[128,1024]{1,0:T(8,128)S(1)}, f32[64,1024]{1,0:T(8,128)S(1)}, f32[128,1024]{1,0:T(8,128)S(1)}, f32[64,1024]{1,0...) custom-call(f32[448,1024]{1,0:T(8,128)S(1)} %rest.1.x_ref, ...), custom_call_target="tpu_custom_call" | custom-call | flops 1000 | bytes 1000 | tf_op jit(solution)/shard_map/own_far/pallas_call | solution.py:266
  11.0 0.0 collective-permute-done.got_ref
  11.0 0.6 collective-permute-start.3
  11.6 1.5 %collective-permute-start.6 = (f32[64,1024]{1,0:T(8,128)S(1)}, f32[64,1024]{1,0:T(8,128)S(1)}, u32[]{:S(2)}, u32[]{:S(2)}) collective-permute-start(f32[64,1024]{1,0:T(8,128)S(1)} %get-tuple-element.31), channel_id=1, source_target_pairs={{0,2},{2,0},{4,6},{6,4},{8,10},{10,8},{12,14},{14,12},{16,18},{18,... | collective-permute-start | bytes 786440 | tf_op jit(solution)/shard_map/ppermute | solution.py:276
  13.1 2.0 %last.1 = f32[512,128]{1,0:T(8,128)} custom-call(f32[64,1024]{1,0:T(8,128)S(1)} %collective-permute-done.got_ref, bf16[512,1024]{1,0:T(8,128)(2,1)S(1)} %get-tuple-element.19.high0_ref, bf16[512,1024]{1,0:T(8,128)(2,1)S(1)} %get-tuple-element.20.low0_ref, bf16[512,1024]{1,0:T(8,128)(2,1)S(1)} %get-tuple-element.22.high1_ref, ...), custom_call_target="tpu_custom_call" | custom-call | flops 1000 | bytes 1000 | tf_op jit(solution)/shard_map/last/pallas_call | solution.py:297
  15.1 11.0 %all-to-all-start = ((f32[16,32,128]{2,1,0:T(8,128)}), f32[16,32,128]{2,1,0:T(8,128)S(1)}, u32[]{:S(2)}, u32[]{:S(2)}) async-start(f32[16,32,128]{2,1,0:T(8,128)} %bitcast.1), calls=%async_computation | async-start | bytes 524288 | tf_op jit(solution)/shard_map/all_to_all | solution.py:286
  26.2 0.0 collective-permute-done.3.got_ref
  26.2 0.3 add_moved.1
  26.5 1.4 %collective-permute-start.4 = (f32[512,128]{1,0:T(8,128)S(1)}, f32[512,128]{1,0:T(8,128)S(1)}, u32[]{:S(2)}, u32[]{:S(2)}) collective-permute-start(f32[512,128]{1,0:T(8,128)S(1)} %get-tuple-element.29), channel_id=1, source_target_pairs={{0,8},{2,10},{4,12},{6,14},{8,16},{10,18},{12,20},{14,22},{16,24},... | collective-permute-start | bytes 786440 | tf_op jit(solution)/shard_map/ppermute | solution.py:283
  27.9 0.7 %collective-permute-start.5 = (f32[512,128]{1,0:T(8,128)S(1)}, f32[512,128]{1,0:T(8,128)S(1)}, u32[]{:S(2)}, u32[]{:S(2)}) collective-permute-start(f32[512,128]{1,0:T(8,128)S(1)} %get-tuple-element.30), channel_id=1, source_target_pairs={{0,24},{2,26},{4,28},{6,30},{8,0},{10,2},{12,4},{14,6},{16,8},{18,... | collective-permute-start | bytes 786440 | tf_op jit(solution)/shard_map/ppermute | solution.py:283
  28.6 2.2 %collective-permute-done.6.got_ref = f32[64,1024]{1,0:T(8,128)S(1)} collective-permute-done((f32[64,1024]{1,0:T(8,128)S(1)}, f32[64,1024]{1,0:T(8,128)S(1)}, u32[]{:S(2)}, u32[]{:S(2)}) %collective-permute-start.6) | collective-permute-done | bytes 262176 | tf_op jit(solution)/shard_map/ppermute | solution.py:276
  30.8 0.2 add_own.1.refs_2_
  31.0 2.9 %collective-permute-done.4.refs_0_ = f32[512,128]{1,0:T(8,128)S(1)} collective-permute-done((f32[512,128]{1,0:T(8,128)S(1)}, f32[512,128]{1,0:T(8,128)S(1)}, u32[]{:S(2)}, u32[]{:S(2)}) %collective-permute-start.4) | collective-permute-done | bytes 262176 | tf_op jit(solution)/shard_map/ppermute | solution.py:283
  33.9 1.0 %collective-permute-done.5.refs_1_ = f32[512,128]{1,0:T(8,128)S(1)} collective-permute-done((f32[512,128]{1,0:T(8,128)S(1)}, f32[512,128]{1,0:T(8,128)S(1)}, u32[]{:S(2)}, u32[]{:S(2)}) %collective-permute-start.5) | collective-permute-done | bytes 262176 | tf_op jit(solution)/shard_map/ppermute | solution.py:283
  34.9 0.9 %gather.1 = f32[1536,128]{1,0:T(8,128)} custom-call(f32[512,128]{1,0:T(8,128)S(1)} %collective-permute-done.4.refs_0_, f32[512,128]{1,0:T(8,128)S(1)} %collective-permute-done.5.refs_1_, f32[512,128]{1,0:T(8,128)S(1)} %add_own.1.refs_2_), custom_call_target="tpu_custom_call" | custom-call | flops 1000 | bytes 1000 | tf_op jit(solution)/shard_map/gather/pallas_call | solution.py:301
  35.8 0.0 all-to-all-done
  35.8 10.3 %all-to-all-start.1 = ((f32[16,96,128]{2,1,0:T(8,128)}), f32[16,96,128]{2,1,0:T(8,128)S(1)}, u32[]{:S(2)}, u32[]{:S(2)}) async-start(f32[16,96,128]{2,1,0:T(8,128)} %bitcast.3), calls=%async_computation.1 | async-start | bytes 1572864 | tf_op jit(solution)/shard_map/all_to_all | solution.py:286
  46.2 0.6 collective-permute-start.2
  46.8 7.3 %collective-permute-done.2.moved_ref = f32[512,128]{1,0:T(8,128)S(1)} collective-permute-done((f32[512,128]{1,0:T(8,128)S(1)}, f32[512,128]{1,0:T(8,128)S(1)}, u32[]{:S(2)}, u32[]{:S(2)}) %collective-permute-start.2) | collective-permute-done | bytes 262176 | tf_op jit(solution)/shard_map/ppermute | solution.py:283
  54.1 10.6 %all-to-all-done.1 = f32[16,96,128]{2,1,0:T(8,128)S(1)} async-done(((f32[16,96,128]{2,1,0:T(8,128)}), f32[16,96,128]{2,1,0:T(8,128)S(1)}, u32[]{:S(2)}, u32[]{:S(2)}) %all-to-all-start.1) | async-done | bytes 786464 | tf_op jit(solution)/shard_map/all_to_all | solution.py:286
  64.6 1.1 %merge.1 = f32[2048,128]{1,0:T(8,128)} custom-call(f32[512,128]{1,0:T(8,128)S(1)} %collective-permute-done.2.moved_ref, f32[1536,128]{1,0:T(8,128)S(1)} %bitcast.10), custom_call_target="tpu_custom_call" | custom-call | flops 1000 | bytes 1000 | tf_op jit(solution)/shard_map/merge/pallas_call | solution.py:304
Async XLA Ops:
  0.0 8.4 %collective-permute-start.1 = (f32[2,512,1024]{2,1,0:T(8,128)}, f32[2,512,1024]{2,1,0:T(8,128)S(1)}, u32[]{:S(2)}, u32[]{:S(2)}) collective-permute-start(f32[2,512,1024]{2,1,0:T(8,128)} %w_ref.1), channel_id=1, source_target_pairs={{0,1},{1,0},{2,3},{3,2},{4,5},{5,4},{6,7},{7,6},{8,9},{9,8},{10,11... | collective-permute-start | bytes 12582920 | tf_op jit(solution)/shard_map/ppermute | solution.py:234
  1.2 9.8 %collective-permute-start = (f32[64,1024]{1,0:T(8,128)S(1)}, f32[64,1024]{1,0:T(8,128)S(1)}, u32[]{:S(2)}, u32[]{:S(2)}) collective-permute-start(f32[64,1024]{1,0:T(8,128)S(1)} %first.1.after_ref), channel_id=1, source_target_pairs={{0,2},{2,0},{4,6},{6,4},{8,10},{10,8},{12,14},{14,12},{16,18},{18,... | collective-permute-start | bytes 786440 | tf_op jit(solution)/shard_map/ppermute | solution.py:248
  11.0 15.1 %collective-permute-start.3 = (f32[128,1024]{1,0:T(8,128)S(1)}, f32[128,1024]{1,0:T(8,128)S(1)}, u32[]{:S(2)}, u32[]{:S(2)}) collective-permute-start(f32[128,1024]{1,0:T(8,128)S(1)} %get-tuple-element.27), channel_id=1, source_target_pairs={{0,2},{2,0},{4,6},{6,4},{8,10},{10,8},{12,14},{14,12},{16,18},{18,... | collective-permute-start | bytes 1572872 | tf_op jit(solution)/shard_map/ppermute | solution.py:275
  11.6 19.1 %collective-permute-start.6 = (f32[64,1024]{1,0:T(8,128)S(1)}, f32[64,1024]{1,0:T(8,128)S(1)}, u32[]{:S(2)}, u32[]{:S(2)}) collective-permute-start(f32[64,1024]{1,0:T(8,128)S(1)} %get-tuple-element.31), channel_id=1, source_target_pairs={{0,2},{2,0},{4,6},{6,4},{8,10},{10,8},{12,14},{14,12},{16,18},{18,... | collective-permute-start | bytes 786440 | tf_op jit(solution)/shard_map/ppermute | solution.py:276
  15.1 20.7 %all-to-all-start = ((f32[16,32,128]{2,1,0:T(8,128)}), f32[16,32,128]{2,1,0:T(8,128)S(1)}, u32[]{:S(2)}, u32[]{:S(2)}) async-start(f32[16,32,128]{2,1,0:T(8,128)} %bitcast.1), calls=%async_computation | async-start | bytes 524288 | tf_op jit(solution)/shard_map/all_to_all | solution.py:286
  26.5 7.4 %collective-permute-start.4 = (f32[512,128]{1,0:T(8,128)S(1)}, f32[512,128]{1,0:T(8,128)S(1)}, u32[]{:S(2)}, u32[]{:S(2)}) collective-permute-start(f32[512,128]{1,0:T(8,128)S(1)} %get-tuple-element.29), channel_id=1, source_target_pairs={{0,8},{2,10},{4,12},{6,14},{8,16},{10,18},{12,20},{14,22},{16,24},... | collective-permute-start | bytes 786440 | tf_op jit(solution)/shard_map/ppermute | solution.py:283
  27.9 7.0 %collective-permute-start.5 = (f32[512,128]{1,0:T(8,128)S(1)}, f32[512,128]{1,0:T(8,128)S(1)}, u32[]{:S(2)}, u32[]{:S(2)}) collective-permute-start(f32[512,128]{1,0:T(8,128)S(1)} %get-tuple-element.30), channel_id=1, source_target_pairs={{0,24},{2,26},{4,28},{6,30},{8,0},{10,2},{12,4},{14,6},{16,8},{18,... | collective-permute-start | bytes 786440 | tf_op jit(solution)/shard_map/ppermute | solution.py:283
  35.8 28.8 %all-to-all-start.1 = ((f32[16,96,128]{2,1,0:T(8,128)}), f32[16,96,128]{2,1,0:T(8,128)S(1)}, u32[]{:S(2)}, u32[]{:S(2)}) async-start(f32[16,96,128]{2,1,0:T(8,128)} %bitcast.3), calls=%async_computation.1 | async-start | bytes 1572864 | tf_op jit(solution)/shard_map/all_to_all | solution.py:286
  46.2 7.9 %collective-permute-start.2 = (f32[512,128]{1,0:T(8,128)S(1)}, f32[512,128]{1,0:T(8,128)S(1)}, u32[]{:S(2)}, u32[]{:S(2)}) collective-permute-start(f32[512,128]{1,0:T(8,128)S(1)} %bitcast.12), channel_id=1, source_target_pairs={{0,16},{2,18},{4,20},{6,22},{8,24},{10,26},{12,28},{14,30},{16,0},... | collective-permute-start | bytes 786440 | tf_op jit(solution)/shard_map/ppermute | solution.py:283

commit v4 on v3

--- a/solution.py
+++ b/solution.py
@@ -12,11 +12,12 @@
 Y = 4
 Z = 8
 R = 4
-FIRST = 2
-MOVED = (1, 3)
-SECOND = MOVED + (0,)
+ALL, LOW, HIGH = (0, 1, 2, 3), (0, 1), (2, 3)
+FIRST = ((2, ALL), (3, LOW))
+MOVED = ((1, ALL), (3, HIGH))
+OWN = ((0, ALL),)
+SECOND = MOVED + OWN
 PARTS = 4
-PIECE = 2 * R * Z
 ADD_FLOPS = 10**11
 START_Z = 5
 
@@ -31,6 +32,10 @@
 
 def in_hbm(value):
     return pltpu.with_memory_space_constraint(value, pltpu.HBM)
+
+
+def count(pieces):
+    return sum(2 * Z * len(rs) for _, rs in pieces)
 
 
 def here():
@@ -49,7 +54,9 @@
 
 
 def product(a_high, a_low, b_high, b_low):
-    return dot(a_high, b_high) + (dot(a_high, b_low) + dot(a_low, b_high))
+    rows = a_high.shape[0]
+    both = dot(jnp.concatenate([a_high, a_low], axis=0), b_high)
+    return both[:rows] + (both[rows:] + dot(a_high, b_low))
 
 
 def tile_rows(mask_ref, shift, width):
@@ -64,27 +71,33 @@
     tiles = width // LANES
     x, y, blk = here()
     partner = x + 1 - 2 * lax.rem(x, 2)
-    mask_copy = pltpu.make_async_copy(mask_ref.at[0], mask_held, sems.at[tiles])
+    mask_copy = pltpu.make_async_copy(mask_ref.at[0], mask_held, sems.at[len(FIRST) * tiles])
     mask_copy.start()
     copies = []
     for t in range(tiles):
         lanes = pl.multiple_of(lax.rem(t + blk * (tiles // 2), tiles) * LANES, LANES)
-        copy = pltpu.make_async_copy(
-            t_ref.at[:, lax.rem(y + FIRST, Y), :, pl.ds(lanes, LANES)], held_ref.at[t], sems.at[t]
-        )
-        copy.start()
-        copies.append(copy)
+        for n, (dy, _) in enumerate(FIRST):
+            copy = pltpu.make_async_copy(
+                t_ref.at[:, lax.rem(y + dy, Y), :, pl.ds(lanes, LANES)],
+                held_ref.at[t, n],
+                sems.at[t * len(FIRST) + n],
+            )
+            copy.start()
+            copies.append(copy)
     mask_copy.wait()
     mask = tile_rows(mask_held, blk * (mask_ref.shape[2] // 2), width)
     for t in range(tiles):
         cols = pl.ds(t * LANES, LANES)
         m = mask[:, t * LANES : (t + 1) * LANES]
-        copies[t].wait()
-        rows = held_ref.at[t].reshape(Z * X * R, LANES)
-        for r in range(R):
-            for h in range(2):
-                value = rows[pl.ds(end(partner, h) * R + r, Z, X * R), :]
-                out_ref[pl.ds((r * 2 + h) * Z, Z), cols] = value * m
+        at = 0
+        for n, (_, rs) in enumerate(FIRST):
+            copies[t * len(FIRST) + n].wait()
+            rows = held_ref.at[t, n].reshape(Z * X * R, LANES)
+            for r in rs:
+                for h in range(2):
+                    value = rows[pl.ds(end(partner, h) * R + r, Z, X * R), :]
+                    out_ref[pl.ds(at, Z), cols] = value * m
+                    at += Z
 
 
 def end(x, h):
@@ -108,17 +121,18 @@
         copies.append(copy)
     mask_copy.wait()
     mask = tile_rows(mask_held, 0, width)
-    wanted = [(dy, x) for dy in (FIRST,) + SECOND] + [(dy, partner) for dy in SECOND]
+    wanted = [(piece, x) for piece in FIRST + SECOND] + [(piece, partner) for piece in SECOND]
     for t in range(tiles):
         copies[t].wait()
         cols = pl.ds(t * LANES, LANES)
         m = mask[:, t * LANES : (t + 1) * LANES]
-        for n, (dy, device) in enumerate(wanted):
-            for h in range(2):
-                base = (lax.rem(y + dy, Y) * X + end(device, h)) * R
-                for r in range(R):
-                    value = held_ref[t, pl.ds(base + r, Z, plane), :]
-                    rest_ref[pl.ds(n * PIECE + (r * 2 + h) * Z, Z), cols] = value * m
+        at = 0
+        for (dy, rs), device in wanted:
+            for r in rs:
+                for h in range(2):
+                    base = (lax.rem(y + dy, Y) * X + end(device, h)) * R
+                    rest_ref[pl.ds(at, Z), cols] = held_ref[t, pl.ds(base + r, Z, plane), :] * m
+                    at += Z
 
 
 def own_kernel(has_first, x_ref, w_ref, *refs):
@@ -164,46 +178,74 @@
     total = part_ref[...]
     for n, (high_ref, low_ref) in enumerate(((high0_ref, low0_ref), (high1_ref, low1_ref))):
         total = total + product(*split(got_ref[:, n * depth : (n + 1) * depth]), high_ref[...], low_ref[...])
-    put(out_ref, total)
-
-
-def put(out_ref, total):
+    put([out_ref], total, FIRST, True)
+
+
+def put(out_refs, total, pieces, joined):
     tiles = total.shape[1] // LANES
-    block = R * tiles
-    for r in range(R):
-        for h in range(2):
-            row = (r * 2 + h) * Z
-            for t in range(tiles):
-                rows = total[row : row + Z, t * LANES : (t + 1) * LANES]
-                out_ref[pl.ds(h * block + t * R + r, Z, 2 * block), :] = pltpu.roll(rows, Z - START_Z, 0)
-
-
-def add_kernel(got_ref, part_ref, *out_refs):
-    for n, out_ref in enumerate(out_refs):
-        rows = pl.ds(n * PIECE, PIECE)
-        put(out_ref, got_ref[rows, :] + part_ref[rows, :])
+    whole = sum(len(rs) for _, rs in pieces) * tiles
+    row, start = 0, 0
+    for n, (_, rs) in enumerate(pieces):
+        out_ref = out_refs[0 if joined else n]
+        block = whole if joined else len(rs) * tiles
+        for j in range(len(rs)):
+            for h in range(2):
+                for t in range(tiles):
+                    rows = pltpu.roll(total[row : row + Z, t * LANES : (t + 1) * LANES], Z - START_Z, 0)
+                    out_ref[pl.ds(h * block + start + t * len(rs) + j, Z, 2 * block), :] = rows
+                row += Z
+        start += len(rs) * tiles if joined else 0
+
+
+def moved_kernel(got_ref, part_ref, *out_refs):
+    put(out_refs, got_ref[...] + part_ref[...], MOVED, False)
+
+
+def own_sum_kernel(got_ref, part_ref, *out_refs):
+    put(out_refs, got_ref[...] + part_ref[...], OWN, False)
+
+
+def turn_kernel(in_ref, *out_refs):
+    whole, start = in_ref.shape[0] // (2 * Z), 0
+    for out_ref in out_refs:
+        block = out_ref.shape[0] // (2 * Z)
+        for n in range(2 * Z):
+            out_ref[pl.ds(n * block, block), :] = in_ref[pl.ds(n * whole + start, block), :]
+        start += block
 
 
 def gather_kernel(*refs):
     *in_refs, out_ref = refs
-    block = in_refs[0].shape[0] // (2 * Z)
-    for j, in_ref in enumerate(in_refs):
+    whole, start = out_ref.shape[0] // (2 * Z), 0
+    for in_ref in in_refs:
+        block = in_ref.shape[0] // (2 * Z)
         for n in range(2 * Z):
-            out_ref[pl.ds((n * len(in_refs) + j) * block, block), :] = in_ref[pl.ds(n * block, block), :]
-
-
-def merge_kernel(moved_ref, second_ref, out_ref):
+            out_ref[pl.ds(n * whole + start, block), :] = in_ref[pl.ds(n * block, block), :]
+        start += block
+
+
+def merge_kernel(*refs):
+    *moved_refs, second_ref, out_ref = refs
     block = out_ref.shape[0] // (2 * Y * Z)
+    tiles = block // R
+    whole = second_ref.shape[0] // (2 * Z)
     _, here_y, _ = here()
-    for dy in range(Y):
+    sources = [(dy, rs, ref, len(rs) * tiles, 0) for (dy, rs), ref in zip(FIRST, moved_refs)]
+    start = 0
+    for dy, rs in SECOND:
+        sources.append((dy, rs, second_ref, whole, start))
+        start += len(rs) * tiles
+    for dy, rs, ref, pitch, start in sources:
         y = lax.rem(here_y - dy + Y, Y)
         for n in range(2 * Z):
-            if dy == FIRST:
-                value = moved_ref[pl.ds(n * block, block), :]
+            z, h = (n // 2 + START_Z) % Z, n % 2
+            to = pl.multiple_of(((z * Y + y) * 2 + h) * block, block)
+            at = n * pitch + start
+            if len(rs) == R:
+                out_ref[pl.ds(to, block), :] = ref[pl.ds(at, block), :]
             else:
-                value = second_ref[pl.ds((n * len(SECOND) + SECOND.index(dy)) * block, block), :]
-            z, h = (n // 2 + START_Z) % Z, n % 2
-            out_ref[pl.ds(pl.multiple_of(((z * Y + y) * 2 + h) * block, block), block), :] = value
+                for j, r in enumerate(rs):
+                    out_ref[pl.ds(to + r, tiles, R), :] = ref[pl.ds(at + j, tiles, len(rs)), :]
 
 
 def call(kernel, name, out_shape, in_specs, scratch=(), flops=1000):
@@ -233,23 +275,24 @@
     swap = [(p, p ^ 1) for p in range(n_pair)]
     other = lax.ppermute(integrals, "blk", [(0, 1), (1, 0)])
     n_tiles = width // LANES
+    n_rest = count(FIRST) + 2 * count(SECOND)
     mask_scratch = pltpu.VMEM(domain_mask.shape[1:], jnp.int32)
     send0 = call(
         first_kernel,
         "first",
-        of(PIECE, width),
+        of(count(FIRST), width),
         [hbm(), hbm()],
         [
-            pltpu.VMEM((n_tiles, Z, X * R, LANES), f32),
+            pltpu.VMEM((n_tiles, len(FIRST), Z, X * R, LANES), f32),
             mask_scratch,
-            pltpu.SemaphoreType.DMA((n_tiles + 1,)),
+            pltpu.SemaphoreType.DMA((len(FIRST) * n_tiles + 1,)),
         ],
     )(in_hbm(amplitudes.reshape(Z, Y, X * R, width)), in_hbm(domain_mask))
     got0 = lax.ppermute(send0, "pair", swap)
     rest = call(
         rest_kernel,
         "rest",
-        of(7 * PIECE, width),
+        of(n_rest, width),
         [hbm(), hbm(), pl.BlockSpec(memory_space=pl.ANY)],
         [pltpu.VMEM((n_tiles, rows, LANES), f32), mask_scratch, pltpu.SemaphoreType.DMA((n_tiles + 1,))],
     )(in_hbm(amplitudes), in_hbm(domain_mask), send0)
@@ -259,19 +302,18 @@
     part, high0, low0 = call(
         functools.partial(own_kernel, False),
         "own_near",
-        [of(7 * PIECE, columns)] + halves_w,
+        [of(n_rest, columns)] + halves_w,
         [vmem(), hbm()],
         scratch,
     )(rest, in_hbm(integrals))
     part0, *parts, high1, low1 = call(
         functools.partial(own_kernel, True),
         "own_far",
-        [of(n * PIECE, columns) for n in (1, 2, 1, 2, 1)] + halves_w,
+        [of(count(pieces), columns) for pieces in (FIRST, MOVED, OWN, MOVED, OWN)] + halves_w,
         [vmem(), hbm(), vmem()],
         scratch,
     )(rest, other, part)
     part_moved, part_own, send_moved, send_own = parts
-    send_moved, send_own, _ = lax.optimization_barrier((send_moved, send_own, got0))
     got_moved = lax.ppermute(send_moved, "pair", swap)
     got_own = lax.ppermute(send_own, "pair", swap)
 
@@ -293,15 +335,22 @@
         )
         return out.reshape(-1, LANES)
 
-    piece = of(PIECE * tiles, LANES)
-    back0 = across(call(last_kernel, "last", piece, [vmem()] * 6)(got0, high0, low0, high1, low1, part0))
-    values = call(add_kernel, "add_moved", [piece] * 2, [vmem()] * 2)(got_moved, part_moved)
-    pieces = [along_y(value, dy) for value, dy in zip(values, MOVED)]
-    pieces += call(add_kernel, "add_own", [piece], [vmem()] * 2, (), ADD_FLOPS)(got_own, part_own)
-    block1 = call(gather_kernel, "gather", of(len(SECOND) * PIECE * tiles, LANES), [vmem()] * len(pieces))(*pieces)
+
+    def blocks(pieces):
+        return [of(count((piece,)) * tiles, LANES) for piece in pieces]
+
+    block0 = call(last_kernel, "last", of(count(FIRST) * tiles, LANES), [vmem()] * 6)(
+        got0, high0, low0, high1, low1, part0
+    )
+    back0 = across(block0)
+    pieces = call(moved_kernel, "add_moved", blocks(MOVED), [vmem()] * 2)(got_moved, part_moved)
+    pieces = [along_y(value, dy) for value, (dy, _) in zip(pieces, MOVED)]
+    pieces += call(own_sum_kernel, "add_own", blocks(OWN), [vmem()] * 2, (), ADD_FLOPS)(got_own, part_own)
+    block1 = call(gather_kernel, "gather", of(count(SECOND) * tiles, LANES), [vmem()] * len(pieces))(*pieces)
     back1 = across(block1)
-    moved = along_y(back0, FIRST)
-    whole = call(merge_kernel, "merge", of(dests * R * tiles, LANES), [vmem()] * 2)(moved, back1)
+    moved = call(turn_kernel, "turn", blocks(FIRST), [vmem()])(back0)
+    moved = [along_y(value, dy) for value, (dy, _) in zip(moved, FIRST)]
+    whole = call(merge_kernel, "merge", of(dests * R * tiles, LANES), [vmem()] * (len(moved) + 1))(*moved, back1)
     return whole.reshape(dests, tiles, R, LANES).transpose(0, 2, 1, 3).reshape(dests, R, columns)
 
 

time: 66.5 us -> 64.5 us (0.970)
  waiting for transfers between devices: 24 us -> 22.8 us
    all_to_all x2, starting transfers between devices: 21.4 us -> 18 us  [across(): lax.all_to_all(block.reshape(2 * Z, -1, LANES), 'pair', split_axis=0, con...]
    ppermute x3 -> x4, starting transfers between devices: 2.73 us -> 5.83 us  [along_y(): return lax.ppermute(value, 'pair', perm)]
    ppermute x1, waiting for transfers between devices: 2.18 us -> 0.01 us  [on_device(): got_own = lax.ppermute(send_own, 'pair', swap)]
    ppermute x3 -> x4, waiting for transfers between devices: 11.2 us -> 12.3 us  [along_y(): return lax.ppermute(value, 'pair', perm)]
    pallas_call x9 -> x10, Pallas kernels: 13.8 us -> 13.5 us  [the longest x1 3.39 us: on_device(): call(functools.partial(own_kernel, False), 'own_near', [of(n_rest, column...]
  transfers between devices with their start and end apart: 9 -> 10, of which waited for: 5 -> 5; matrix products, arithmetic and copies ran while one was open for 0% -> 0% of each run, Pallas kernels for 19% -> 19%
where the time goes in v4:
time: 64.5 us; the launch traced here: 63.9 us
  starting transfers between devices  27.5 us (43%)
  waiting for transfers between devices  22.8 us (35%)
  Pallas kernels  13.5 us (21%)
    all_to_all x2, starting transfers between devices, across(): lax.all_to_all(block.reshape(2 * Z, -1, LANES), 'pair', split_axis=0, con...  18 us
    ppermute x4, waiting for transfers between devices, along_y(): return lax.ppermute(value, 'pair', perm)  12.3 us
    all_to_all x2, waiting for transfers between devices, across(): lax.all_to_all(block.reshape(2 * Z, -1, LANES), 'pair', split_axis=0, con...  10.5 us
    ppermute x4, starting transfers between devices, along_y(): return lax.ppermute(value, 'pair', perm)  5.83 us
    pallas_call x1, Pallas kernels, on_device(): call(functools.partial(own_kernel, False), 'own_near', [of(n_rest, column...  3.39 us
    pallas_call x1, Pallas kernels, on_device(): call(functools.partial(own_kernel, True), 'own_far', [of(count(pieces), c...  2.45 us
    pallas_call x1, Pallas kernels, on_device(): call(rest_kernel, 'rest', of(n_rest, width), [hbm(), hbm(), pl.BlockSpec(...  2.08 us
    pallas_call x1, Pallas kernels, on_device(): call(last_kernel, 'last', of(count(FIRST) * tiles, LANES), [vmem()] * 6)  1.79 us
  transfers between devices with their start and end apart: 10, of which 5 were waited for; matrix products, arithmetic and copies ran while one was open for 0% of the time, Pallas kernels for 19%

profile of v4, /device:TPU:16, one launch (start us, length us, event | category | flops | bytes accessed | tf_op | source)
XLA Modules:
  0.0 63.9 jit_solution(4992258815079990572)
XLA Ops:
  0.0 0.0 collective-permute-start.1
  0.0 1.4 %first.1.after_ref = f32[96,1024]{1,0:T(8,128)S(1)} custom-call(f32[8,4,16,1024]{3,2,1,0:T(8,128)} %bitcast.12, s32[1,8,16]{2,1,0:T(8,128)} %mask_ref.3), custom_call_target="tpu_custom_call" | custom-call | flops 1000 | bytes 1000 | tf_op jit(solution)/shard_map/first/pallas_call | solution.py:280
  1.4 1.6 %collective-permute-start = (f32[96,1024]{1,0:T(8,128)S(1)}, f32[96,1024]{1,0:T(8,128)S(1)}, u32[]{:S(2)}, u32[]{:S(2)}) collective-permute-start(f32[96,1024]{1,0:T(8,128)S(1)} %first.1.after_ref), channel_id=1, source_target_pairs={{0,2},{2,0},{4,6},{6,4},{8,10},{10,8},{12,14},{14,12},{16,18},{18,... | collective-permute-start | bytes 1179656 | tf_op jit(solution)/shard_map/ppermute | solution.py:291
  3.0 2.1 %rest.1.x_ref = f32[416,1024]{1,0:T(8,128)S(1)} custom-call(f32[1,512,1024]{2,1,0:T(8,128)} %t_ref.1, s32[1,8,16]{2,1,0:T(8,128)} %mask_ref.3, f32[96,1024]{1,0:T(8,128)S(1)} %first.1.after_ref), custom_call_target="tpu_custom_call" | custom-call | flops 1000 | bytes 1000 | tf_op jit(solution)/shard_map/rest/pallas_call | solution.py:292
  5.1 3.4 %own_near.1 = (f32[416,1024]{1,0:T(8,128)S(1)}, bf16[512,1024]{1,0:T(8,128)(2,1)S(1)}, bf16[512,1024]{1,0:T(8,128)(2,1)S(1)}) custom-call(f32[416,1024]{1,0:T(8,128)S(1)} %rest.1.x_ref, f32[2,512,1024]{2,1,0:T(8,128)} %w_ref.1), custom_call_target="tpu_custom_call" | custom-call | flops 1000 | bytes 1000 | tf_op jit(solution)/shard_map/own_near/pallas_call | solution.py:302
  8.5 0.0 collective-permute-done.1.w_ref
  8.5 2.4 %own_far.1 = (f32[96,1024]{1,0:T(8,128)S(1)}, f32[96,1024]{1,0:T(8,128)S(1)}, f32[64,1024]{1,0:T(8,128)S(1)}, f32[96,1024]{1,0:T(8,128)S(1)}, f32[64,1024]{1,0:T...) custom-call(f32[416,1024]{1,0:T(8,128)S(1)} %rest.1.x_ref, ...), custom_call_target="tpu_custom_call" | custom-call | flops 1000 | bytes 1000 | tf_op jit(solution)/shard_map/own_far/pallas_call | solution.py:309
  11.0 0.6 collective-permute-start.4
  11.6 1.5 %collective-permute-start.7 = (f32[64,1024]{1,0:T(8,128)S(1)}, f32[64,1024]{1,0:T(8,128)S(1)}, u32[]{:S(2)}, u32[]{:S(2)}) collective-permute-start(f32[64,1024]{1,0:T(8,128)S(1)} %get-tuple-element.31), channel_id=1, source_target_pairs={{0,2},{2,0},{4,6},{6,4},{8,10},{10,8},{12,14},{14,12},{16,18},{18,... | collective-permute-start | bytes 786440 | tf_op jit(solution)/shard_map/ppermute | solution.py:318
  13.1 0.0 collective-permute-done.got_ref
  13.1 1.8 %last.1 = f32[768,128]{1,0:T(8,128)} custom-call(f32[96,1024]{1,0:T(8,128)S(1)} %collective-permute-done.got_ref, bf16[512,1024]{1,0:T(8,128)(2,1)S(1)} %get-tuple-element.19.high0_ref, bf16[512,1024]{1,0:T(8,128)(2,1)S(1)} %get-tuple-element.20.low0_ref, bf16[512,1024]{1,0:T(8,128)(2,1)S(1)} %get-tuple-element.22.high1_ref, ...), custom_call_target="tpu_custom_call" | custom-call | flops 1000 | bytes 1000 | tf_op jit(solution)/shard_map/last/pallas_call | solution.py:342
  14.9 11.7 %all-to-all-start = ((f32[16,48,128]{2,1,0:T(8,128)}), f32[16,48,128]{2,1,0:T(8,128)S(1)}, u32[]{:S(2)}, u32[]{:S(2)}) async-start(f32[16,48,128]{2,1,0:T(8,128)} %bitcast.1), calls=%async_computation | async-start | bytes 786432 | tf_op jit(solution)/shard_map/all_to_all | solution.py:328
  26.5 0.0 collective-permute-done.4.got_ref
  26.5 0.2 add_moved.1
  26.8 0.5 collective-permute-start.6
  27.3 1.6 %collective-permute-start.5 = (f32[512,128]{1,0:T(8,128)S(1)}, f32[512,128]{1,0:T(8,128)S(1)}, u32[]{:S(2)}, u32[]{:S(2)}) collective-permute-start(f32[512,128]{1,0:T(8,128)S(1)} %get-tuple-element.29), channel_id=1, source_target_pairs={{0,8},{2,10},{4,12},{6,14},{8,16},{10,18},{12,20},{14,22},{16,24},... | collective-permute-start | bytes 786440 | tf_op jit(solution)/shard_map/ppermute | solution.py:325
  28.9 0.0 collective-permute-done.7.got_ref
  28.9 0.2 add_own.1.refs_2_
  29.1 2.8 %collective-permute-done.6.refs_1_ = f32[256,128]{1,0:T(8,128)S(1)} collective-permute-done((f32[256,128]{1,0:T(8,128)S(1)}, f32[256,128]{1,0:T(8,128)S(1)}, u32[]{:S(2)}, u32[]{:S(2)}) %collective-permute-start.6) | collective-permute-done | bytes 131104 | tf_op jit(solution)/shard_map/ppermute | solution.py:325
  31.8 2.6 %collective-permute-done.5.refs_0_ = f32[512,128]{1,0:T(8,128)S(1)} collective-permute-done((f32[512,128]{1,0:T(8,128)S(1)}, f32[512,128]{1,0:T(8,128)S(1)}, u32[]{:S(2)}, u32[]{:S(2)}) %collective-permute-start.5) | collective-permute-done | bytes 262176 | tf_op jit(solution)/shard_map/ppermute | solution.py:325
  34.4 0.9 %gather.1 = f32[1280,128]{1,0:T(8,128)} custom-call(f32[512,128]{1,0:T(8,128)S(1)} %collective-permute-done.5.refs_0_, f32[256,128]{1,0:T(8,128)S(1)} %collective-permute-done.6.refs_1_, f32[512,128]{1,0:T(8,128)S(1)} %add_own.1.refs_2_), custom_call_target="tpu_custom_call" | custom-call | flops 1000 | bytes 1000 | tf_op jit(solution)/shard_map/gather/pallas_call | solution.py:349
  35.3 3.5 %all-to-all-done = f32[16,48,128]{2,1,0:T(8,128)S(1)} async-done(((f32[16,48,128]{2,1,0:T(8,128)}), f32[16,48,128]{2,1,0:T(8,128)S(1)}, u32[]{:S(2)}, u32[]{:S(2)}) %all-to-all-start) | async-done | bytes 393248 | tf_op jit(solution)/shard_map/all_to_all | solution.py:328
  38.8 6.3 %all-to-all-start.1 = ((f32[16,80,128]{2,1,0:T(8,128)}), f32[16,80,128]{2,1,0:T(8,128)S(1)}, u32[]{:S(2)}, u32[]{:S(2)}) async-start(f32[16,80,128]{2,1,0:T(8,128)} %bitcast.3), calls=%async_computation.1 | async-start | bytes 1310720 | tf_op jit(solution)/shard_map/all_to_all | solution.py:328
  45.1 3.7 %collective-permute-start.2 = (f32[512,128]{1,0:T(8,128)S(1)}, f32[512,128]{1,0:T(8,128)S(1)}, u32[]{:S(2)}, u32[]{:S(2)}) collective-permute-start(f32[512,128]{1,0:T(8,128)S(1)} %get-tuple-element.25), channel_id=1, source_target_pairs={{0,16},{2,18},{4,20},{6,22},{8,24},{10,26},{12,28},{14,30},{16,0},... | collective-permute-start | bytes 786440 | tf_op jit(solution)/shard_map/ppermute | solution.py:325
  48.9 0.0 collective-permute-start.3
  48.9 6.9 %collective-permute-done.3.refs_1_ = f32[256,128]{1,0:T(8,128)S(1)} collective-permute-done((f32[256,128]{1,0:T(8,128)S(1)}, f32[256,128]{1,0:T(8,128)S(1)}, u32[]{:S(2)}, u32[]{:S(2)}) %collective-permute-start.3) | collective-permute-done | bytes 131104 | tf_op jit(solution)/shard_map/ppermute | solution.py:325
  55.8 0.0 collective-permute-done.2.refs_0_
  55.8 7.0 %all-to-all-done.1 = f32[16,80,128]{2,1,0:T(8,128)S(1)} async-done(((f32[16,80,128]{2,1,0:T(8,128)}), f32[16,80,128]{2,1,0:T(8,128)S(1)}, u32[]{:S(2)}, u32[]{:S(2)}) %all-to-all-start.1) | async-done | bytes 655392 | tf_op jit(solution)/shard_map/all_to_all | solution.py:328
  62.8 1.1 %merge.1 = f32[2048,128]{1,0:T(8,128)} custom-call(f32[512,128]{1,0:T(8,128)S(1)} %collective-permute-done.2.refs_0_, f32[256,128]{1,0:T(8,128)S(1)} %collective-permute-done.3.refs_1_, f32[1280,128]{1,0:T(8,128)S(1)} %bitcast.10), custom_call_target="tpu_custom_call" | custom-call | flops 1000 | bytes 1000 | tf_op jit(solution)/shard_map/merge/pallas_call | solution.py:353
  (1 shorter events, 0.0 us)
Async XLA Ops:
  0.0 8.5 %collective-permute-start.1 = (f32[2,512,1024]{2,1,0:T(8,128)}, f32[2,512,1024]{2,1,0:T(8,128)S(1)}, u32[]{:S(2)}, u32[]{:S(2)}) collective-permute-start(f32[2,512,1024]{2,1,0:T(8,128)} %w_ref.1), channel_id=1, source_target_pairs={{0,1},{1,0},{2,3},{3,2},{4,5},{5,4},{6,7},{7,6},{8,9},{9,8},{10,11... | collective-permute-start | bytes 12582920 | tf_op jit(solution)/shard_map/ppermute | solution.py:276
  1.4 11.6 %collective-permute-start = (f32[96,1024]{1,0:T(8,128)S(1)}, f32[96,1024]{1,0:T(8,128)S(1)}, u32[]{:S(2)}, u32[]{:S(2)}) collective-permute-start(f32[96,1024]{1,0:T(8,128)S(1)} %first.1.after_ref), channel_id=1, source_target_pairs={{0,2},{2,0},{4,6},{6,4},{8,10},{10,8},{12,14},{14,12},{16,18},{18,... | collective-permute-start | bytes 1179656 | tf_op jit(solution)/shard_map/ppermute | solution.py:291
  11.0 15.6 %collective-permute-start.4 = (f32[96,1024]{1,0:T(8,128)S(1)}, f32[96,1024]{1,0:T(8,128)S(1)}, u32[]{:S(2)}, u32[]{:S(2)}) collective-permute-start(f32[96,1024]{1,0:T(8,128)S(1)} %get-tuple-element.27), channel_id=1, source_target_pairs={{0,2},{2,0},{4,6},{6,4},{8,10},{10,8},{12,14},{14,12},{16,18},{18,... | collective-permute-start | bytes 1179656 | tf_op jit(solution)/shard_map/ppermute | solution.py:317
  11.6 17.3 %collective-permute-start.7 = (f32[64,1024]{1,0:T(8,128)S(1)}, f32[64,1024]{1,0:T(8,128)S(1)}, u32[]{:S(2)}, u32[]{:S(2)}) collective-permute-start(f32[64,1024]{1,0:T(8,128)S(1)} %get-tuple-element.31), channel_id=1, source_target_pairs={{0,2},{2,0},{4,6},{6,4},{8,10},{10,8},{12,14},{14,12},{16,18},{18,... | collective-permute-start | bytes 786440 | tf_op jit(solution)/shard_map/ppermute | solution.py:318
  14.9 23.9 %all-to-all-start = ((f32[16,48,128]{2,1,0:T(8,128)}), f32[16,48,128]{2,1,0:T(8,128)S(1)}, u32[]{:S(2)}, u32[]{:S(2)}) async-start(f32[16,48,128]{2,1,0:T(8,128)} %bitcast.1), calls=%async_computation | async-start | bytes 786432 | tf_op jit(solution)/shard_map/all_to_all | solution.py:328
  26.8 5.0 %collective-permute-start.6 = (f32[256,128]{1,0:T(8,128)S(1)}, f32[256,128]{1,0:T(8,128)S(1)}, u32[]{:S(2)}, u32[]{:S(2)}) collective-permute-start(f32[256,128]{1,0:T(8,128)S(1)} %get-tuple-element.30), channel_id=1, source_target_pairs={{0,24},{2,26},{4,28},{6,30},{8,0},{10,2},{12,4},{14,6},{16,8},{18,... | collective-permute-start | bytes 393224 | tf_op jit(solution)/shard_map/ppermute | solution.py:325
  27.3 7.1 %collective-permute-start.5 = (f32[512,128]{1,0:T(8,128)S(1)}, f32[512,128]{1,0:T(8,128)S(1)}, u32[]{:S(2)}, u32[]{:S(2)}) collective-permute-start(f32[512,128]{1,0:T(8,128)S(1)} %get-tuple-element.29), channel_id=1, source_target_pairs={{0,8},{2,10},{4,12},{6,14},{8,16},{10,18},{12,20},{14,22},{16,24},... | collective-permute-start | bytes 786440 | tf_op jit(solution)/shard_map/ppermute | solution.py:325
  38.8 24.0 %all-to-all-start.1 = ((f32[16,80,128]{2,1,0:T(8,128)}), f32[16,80,128]{2,1,0:T(8,128)S(1)}, u32[]{:S(2)}, u32[]{:S(2)}) async-start(f32[16,80,128]{2,1,0:T(8,128)} %bitcast.3), calls=%async_computation.1 | async-start | bytes 1310720 | tf_op jit(solution)/shard_map/all_to_all | solution.py:328
  45.1 10.6 %collective-permute-start.2 = (f32[512,128]{1,0:T(8,128)S(1)}, f32[512,128]{1,0:T(8,128)S(1)}, u32[]{:S(2)}, u32[]{:S(2)}) collective-permute-start(f32[512,128]{1,0:T(8,128)S(1)} %get-tuple-element.25), channel_id=1, source_target_pairs={{0,16},{2,18},{4,20},{6,22},{8,24},{10,26},{12,28},{14,30},{16,0},... | collective-permute-start | bytes 786440 | tf_op jit(solution)/shard_map/ppermute | solution.py:325
  48.9 6.9 %collective-permute-start.3 = (f32[256,128]{1,0:T(8,128)S(1)}, f32[256,128]{1,0:T(8,128)S(1)}, u32[]{:S(2)}, u32[]{:S(2)}) collective-permute-start(f32[256,128]{1,0:T(8,128)S(1)} %get-tuple-element.26), channel_id=1, source_target_pairs={{0,24},{2,26},{4,28},{6,30},{8,0},{10,2},{12,4},{14,6},{16,8},{18,... | collective-permute-start | bytes 393224 | tf_op jit(solution)/shard_map/ppermute | solution.py:325

commit v5 on v4

--- a/solution.py
+++ b/solution.py
@@ -12,11 +12,9 @@
 Y = 4
 Z = 8
 R = 4
-ALL, LOW, HIGH = (0, 1, 2, 3), (0, 1), (2, 3)
-FIRST = ((2, ALL), (3, LOW))
-MOVED = ((1, ALL), (3, HIGH))
-OWN = ((0, ALL),)
-SECOND = MOVED + OWN
+ALL = (0, 1, 2, 3)
+FIRST = ((2, ALL), (0, (0, 1)))
+SECOND = ((1, ALL), (3, ALL), (0, (2, 3)))
 PARTS = 4
 ADD_FLOPS = 10**11
 START_Z = 5
@@ -105,7 +103,9 @@
     return jnp.where(outer, h * (X - 1), 1 + h)
 
 
-def rest_kernel(t_ref, mask_ref, after_ref, rest_ref, held_ref, mask_held, sems):
+def near_kernel(
+    t_ref, mask_ref, w_ref, after_ref, rest_ref, part_ref, high_ref, low_ref, held_ref, mask_held, w_held, sems, w_sems
+):
     del after_ref
     rows, width = t_ref.shape[1:]
     x, y, blk = here()
@@ -119,6 +119,7 @@
         copy = pltpu.make_async_copy(t_ref.at[0, :, pl.ds(t * LANES, LANES)], held_ref.at[t], sems.at[t])
         copy.start()
         copies.append(copy)
+    w_copies = start_weights(w_ref, w_held, w_sems)
     mask_copy.wait()
     mask = tile_rows(mask_held, 0, width)
     wanted = [(piece, x) for piece in FIRST + SECOND] + [(piece, partner) for piece in SECOND]
@@ -133,16 +134,12 @@
                     base = (lax.rem(y + dy, Y) * X + end(device, h)) * R
                     rest_ref[pl.ds(at, Z), cols] = held_ref[t, pl.ds(base + r, Z, plane), :] * m
                     at += Z
-
-
-def own_kernel(has_first, x_ref, w_ref, *refs):
-    x, _, blk = here()
-    k = lax.rem(x, 2)
-    half = 1 - blk if has_first else blk
-    first_ref = refs[0] if has_first else None
-    *part_refs, high_ref, low_ref, held_ref, sems = refs[has_first:]
-    depth = w_ref.shape[1]
-    piece = depth // PARTS
+    contract(w_copies, blk, rest_ref, None, [part_ref], high_ref, low_ref, w_held)
+
+
+def start_weights(w_ref, held_ref, sems):
+    k = lax.rem(here()[0], 2)
+    piece = w_ref.shape[1] // PARTS
     copies = []
     for which, of in enumerate((k, 1 - k)):
         for q in range(PARTS):
@@ -153,24 +150,33 @@
             )
             copy.start()
             copies.append(copy)
-    cols = pl.ds(pl.multiple_of(half * depth, depth), depth)
-    x_high, x_low = split(x_ref[:, cols])
-    total = first_ref[...] if has_first else None
+    return copies
+
+
+def contract(copies, half, x_ref, first_ref, part_refs, high_ref, low_ref, held_ref):
+    depth = held_ref.shape[1]
+    x_high, x_low = split(x_ref[:, pl.ds(pl.multiple_of(half * depth, depth), depth)])
     for copy in copies[:PARTS]:
         copy.wait()
-    w_high, w_low = split(held_ref[0])
-    term = product(x_high, x_low, w_high, w_low)
-    total = term if total is None else total + term
+    total = product(x_high, x_low, *split(held_ref[0]))
+    if first_ref is not None:
+        total = first_ref[...] + total
     base = 0
     for part_ref in part_refs:
-        count = part_ref.shape[0]
-        part_ref[...] = total[base : base + count]
-        base += count
+        size = part_ref.shape[0]
+        part_ref[...] = total[base : base + size]
+        base += size
     for copy in copies[PARTS:]:
         copy.wait()
     o_high, o_low = split(held_ref[1])
     high_ref[...] = o_high
     low_ref[...] = o_low
+
+
+def far_kernel(x_ref, w_ref, first_ref, *refs):
+    *part_refs, high_ref, low_ref, held_ref, sems = refs
+    copies = start_weights(w_ref, held_ref, sems)
+    contract(copies, 1 - here()[2], x_ref, first_ref, part_refs, high_ref, low_ref, held_ref)
 
 
 def last_kernel(got_ref, high0_ref, low0_ref, high1_ref, low1_ref, part_ref, out_ref):
@@ -197,12 +203,8 @@
         start += len(rs) * tiles if joined else 0
 
 
-def moved_kernel(got_ref, part_ref, *out_refs):
-    put(out_refs, got_ref[...] + part_ref[...], MOVED, False)
-
-
-def own_sum_kernel(got_ref, part_ref, *out_refs):
-    put(out_refs, got_ref[...] + part_ref[...], OWN, False)
+def sum_kernel(piece, got_ref, part_ref, out_ref):
+    put([out_ref], got_ref[...] + part_ref[...], (piece,), False)
 
 
 def turn_kernel(in_ref, *out_refs):
@@ -289,33 +291,25 @@
         ],
     )(in_hbm(amplitudes.reshape(Z, Y, X * R, width)), in_hbm(domain_mask))
     got0 = lax.ppermute(send0, "pair", swap)
-    rest = call(
-        rest_kernel,
-        "rest",
-        of(n_rest, width),
-        [hbm(), hbm(), pl.BlockSpec(memory_space=pl.ANY)],
-        [pltpu.VMEM((n_tiles, rows, LANES), f32), mask_scratch, pltpu.SemaphoreType.DMA((n_tiles + 1,))],
-    )(in_hbm(amplitudes), in_hbm(domain_mask), send0)
-
     halves_w = [of(depth, columns, dtype=bf16)] * 2
     scratch = [pltpu.VMEM((2, depth, columns), f32), pltpu.SemaphoreType.DMA((2, PARTS))]
-    part, high0, low0 = call(
-        functools.partial(own_kernel, False),
-        "own_near",
-        [of(n_rest, columns)] + halves_w,
-        [vmem(), hbm()],
-        scratch,
-    )(rest, in_hbm(integrals))
+    rest, part, high0, low0 = call(
+        near_kernel,
+        "near",
+        [of(n_rest, width), of(n_rest, columns)] + halves_w,
+        [hbm(), hbm(), hbm(), pl.BlockSpec(memory_space=pl.ANY)],
+        [pltpu.VMEM((n_tiles, rows, LANES), f32), mask_scratch, scratch[0], pltpu.SemaphoreType.DMA((n_tiles + 1,)), scratch[1]],
+    )(in_hbm(amplitudes), in_hbm(domain_mask), in_hbm(integrals), send0)
+    sizes = [count((piece,)) for piece in SECOND]
     part0, *parts, high1, low1 = call(
-        functools.partial(own_kernel, True),
-        "own_far",
-        [of(count(pieces), columns) for pieces in (FIRST, MOVED, OWN, MOVED, OWN)] + halves_w,
+        far_kernel,
+        "far",
+        [of(n, columns) for n in [count(FIRST)] + sizes + sizes] + halves_w,
         [vmem(), hbm(), vmem()],
         scratch,
     )(rest, other, part)
-    part_moved, part_own, send_moved, send_own = parts
-    got_moved = lax.ppermute(send_moved, "pair", swap)
-    got_own = lax.ppermute(send_own, "pair", swap)
+    parts, sends = parts[: len(SECOND)], parts[len(SECOND) :]
+    got = [lax.ppermute(send, "pair", swap) for send in sends]
 
     def along_y(value, dy):
         perm = []
@@ -343,13 +337,21 @@
         got0, high0, low0, high1, low1, part0
     )
     back0 = across(block0)
-    pieces = call(moved_kernel, "add_moved", blocks(MOVED), [vmem()] * 2)(got_moved, part_moved)
-    pieces = [along_y(value, dy) for value, (dy, _) in zip(pieces, MOVED)]
-    pieces += call(own_sum_kernel, "add_own", blocks(OWN), [vmem()] * 2, (), ADD_FLOPS)(got_own, part_own)
+    pieces = []
+    for n, (dy, rs) in enumerate(SECOND):
+        value = call(
+            functools.partial(sum_kernel, (dy, rs)),
+            "sum",
+            of(sizes[n] * tiles, LANES),
+            [vmem()] * 2,
+            (),
+            1000 if dy else ADD_FLOPS,
+        )(got[n], parts[n])
+        pieces.append(along_y(value, dy) if dy else value)
     block1 = call(gather_kernel, "gather", of(count(SECOND) * tiles, LANES), [vmem()] * len(pieces))(*pieces)
     back1 = across(block1)
-    moved = call(turn_kernel, "turn", blocks(FIRST), [vmem()])(back0)
-    moved = [along_y(value, dy) for value, (dy, _) in zip(moved, FIRST)]
+    moved = call(turn_kernel, "turn", blocks(FIRST), [vmem()])(back0) if len(FIRST) > 1 else [back0]
+    moved = [along_y(value, dy) if dy else value for value, (dy, _) in zip(moved, FIRST)]
     whole = call(merge_kernel, "merge", of(dests * R * tiles, LANES), [vmem()] * (len(moved) + 1))(*moved, back1)
     return whole.reshape(dests, tiles, R, LANES).transpose(0, 2, 1, 3).reshape(dests, R, columns)
 

time: 64.5 us -> 64.2 us (level)
  starting transfers between devices: 27.5 us -> 26.2 us
  waiting for transfers between devices: 22.8 us -> 24 us
  Pallas kernels: 13.5 us -> 12.8 us
    ppermute x4 -> x3, starting transfers between devices: 5.83 us -> 2.9 us  [along_y(): return lax.ppermute(value, 'pair', perm)]
    ppermute x2 -> x3, starting transfers between devices: 2.11 us -> 3.01 us  [on_device(): got = [lax.ppermute(send, 'pair', swap) for send in sends]]
    ppermute x4 -> x3, waiting for transfers between devices: 12.3 us -> 13.1 us  [along_y(): return lax.ppermute(value, 'pair', perm)]
    all_to_all x2, starting transfers between devices: 18 us -> 18.7 us  [across(): lax.all_to_all(block.reshape(2 * Z, -1, LANES), 'pair', split_axis=0, con...]
    pallas_call x6, Pallas kernels: 8.35 us -> 7.7 us  [the longest x1 4.9 us: on_device(): call(near_kernel, 'near', [of(n_rest, width), of(n_rest, columns)] + halv...]
where the time goes in v5:
time: 64.2 us; the launch traced here: 63.1 us
  starting transfers between devices  26.2 us (41%)
  waiting for transfers between devices  24 us (37%)
  Pallas kernels  12.8 us (20%)
    all_to_all x2, starting transfers between devices, across(): lax.all_to_all(block.reshape(2 * Z, -1, LANES), 'pair', split_axis=0, con...  18.7 us
    ppermute x3, waiting for transfers between devices, along_y(): return lax.ppermute(value, 'pair', perm)  13.1 us
    all_to_all x2, waiting for transfers between devices, across(): lax.all_to_all(block.reshape(2 * Z, -1, LANES), 'pair', split_axis=0, con...  10.9 us
    pallas_call x1, Pallas kernels, on_device(): call(near_kernel, 'near', [of(n_rest, width), of(n_rest, columns)] + halv...  4.9 us
    ppermute x3, starting transfers between devices, on_device(): got = [lax.ppermute(send, 'pair', swap) for send in sends]  3.01 us
    ppermute x3, starting transfers between devices, along_y(): return lax.ppermute(value, 'pair', perm)  2.9 us
    pallas_call x1, Pallas kernels, on_device(): call(far_kernel, 'far', [of(n, columns) for n in [count(FIRST)] + sizes +...  2.36 us
    pallas_call x1, Pallas kernels, on_device(): call(last_kernel, 'last', of(count(FIRST) * tiles, LANES), [vmem()] * 6)  1.79 us
  transfers between devices with their start and end apart: 10, of which 5 were waited for; matrix products, arithmetic and copies ran while one was open for 0% of the time, Pallas kernels for 19%

profile of v5, /device:TPU:16, one launch (start us, length us, event | category | flops | bytes accessed | tf_op | source)
XLA Modules:
  0.0 63.1 jit_solution(11841743549482650972)
XLA Ops:
  0.0 0.0 collective-permute-start.1
  0.0 1.4 %first.1.after_ref = f32[96,1024]{1,0:T(8,128)S(1)} custom-call(f32[8,4,16,1024]{3,2,1,0:T(8,128)} %bitcast.12, s32[1,8,16]{2,1,0:T(8,128)} %mask_ref.3), custom_call_target="tpu_custom_call" | custom-call | flops 1000 | bytes 1000 | tf_op jit(solution)/shard_map/first/pallas_call | solution.py:282
  1.4 1.6 %collective-permute-start = (f32[96,1024]{1,0:T(8,128)S(1)}, f32[96,1024]{1,0:T(8,128)S(1)}, u32[]{:S(2)}, u32[]{:S(2)}) collective-permute-start(f32[96,1024]{1,0:T(8,128)S(1)} %first.1.after_ref), channel_id=1, source_target_pairs={{0,2},{2,0},{4,6},{6,4},{8,10},{10,8},{12,14},{14,12},{16,18},{18,... | collective-permute-start | bytes 1179656 | tf_op jit(solution)/shard_map/ppermute | solution.py:293
  3.0 4.9 %near.1 = (f32[416,1024]{1,0:T(8,128)S(1)}, f32[416,1024]{1,0:T(8,128)S(1)}, bf16[512,1024]{1,0:T(8,128)(2,1)S(1)}, bf16[512,1024]{1,0:T(8,128)(2,1)S(1)}) custom-call(f32[1,512,1024]{2,1,0:T(8,128)} %t_ref.1, s32[1,8,16]{2,1,0:T(8,128)} %mask_ref.3, f32[2,512,1024]{2,1,0:T(8,128)} %w_ref.1, f32[96,1024]{1,0:T(8,128)S(1)} %first.1.after_ref), custom_call_target="tpu_custom_call" | custom-call | flops 1000 | bytes 1000 | tf_op jit(solution)/shard_map/near/pallas_call | solution.py:296
  7.9 0.0 collective-permute-done.1.w_ref
  7.9 2.4 %far.1 = (f32[96,1024]{1,0:T(8,128)S(1)}, f32[64,1024]{1,0:T(8,128)S(1)}, f32[64,1024]{1,0:T(8,128)S(1)}, f32[32,1024]{1,0:T(8,128)S(1)}, f32[64,1024]{1,0:T(8,1...) custom-call(f32[416,1024]{1,0:T(8,128)S(1)} %get-tuple-element.22.x_, ...), custom_call_target="tpu_custom_call" | custom-call | flops 1000 | bytes 1000 | tf_op jit(solution)/shard_map/far/pallas_call | solution.py:304
  10.3 1.0 %collective-permute-start.3 = (f32[64,1024]{1,0:T(8,128)S(1)}, f32[64,1024]{1,0:T(8,128)S(1)}, u32[]{:S(2)}, u32[]{:S(2)}) collective-permute-start(f32[64,1024]{1,0:T(8,128)S(1)} %get-tuple-element.29), channel_id=1, source_target_pairs={{0,2},{2,0},{4,6},{6,4},{8,10},{10,8},{12,14},{14,12},{16,18},{18,... | collective-permute-start | bytes 786440 | tf_op jit(solution)/shard_map/ppermute | solution.py:312
  11.3 1.1 %collective-permute-start.5 = (f32[64,1024]{1,0:T(8,128)S(1)}, f32[64,1024]{1,0:T(8,128)S(1)}, u32[]{:S(2)}, u32[]{:S(2)}) collective-permute-start(f32[64,1024]{1,0:T(8,128)S(1)} %get-tuple-element.31), channel_id=1, source_target_pairs={{0,2},{2,0},{4,6},{6,4},{8,10},{10,8},{12,14},{14,12},{16,18},{18,... | collective-permute-start | bytes 786440 | tf_op jit(solution)/shard_map/ppermute | solution.py:312
  12.4 0.9 %collective-permute-start.7 = (f32[32,1024]{1,0:T(8,128)S(1)}, f32[32,1024]{1,0:T(8,128)S(1)}, u32[]{:S(2)}, u32[]{:S(2)}) collective-permute-start(f32[32,1024]{1,0:T(8,128)S(1)} %get-tuple-element.33), channel_id=1, source_target_pairs={{0,2},{2,0},{4,6},{6,4},{8,10},{10,8},{12,14},{14,12},{16,18},{18,... | collective-permute-start | bytes 393224 | tf_op jit(solution)/shard_map/ppermute | solution.py:312
  13.3 0.0 collective-permute-done.got_ref
  13.3 1.8 %last.1 = f32[768,128]{1,0:T(8,128)} custom-call(f32[96,1024]{1,0:T(8,128)S(1)} %collective-permute-done.got_ref, bf16[512,1024]{1,0:T(8,128)(2,1)S(1)} %get-tuple-element.20.high0_ref, bf16[512,1024]{1,0:T(8,128)(2,1)S(1)} %get-tuple-element.21.low0_ref, bf16[512,1024]{1,0:T(8,128)(2,1)S(1)} %get-tuple-element.24.high1_ref, ...), custom_call_target="tpu_custom_call" | custom-call | flops 1000 | bytes 1000 | tf_op jit(solution)/shard_map/last/pallas_call | solution.py:336
  15.1 11.8 %all-to-all-start = ((f32[16,48,128]{2,1,0:T(8,128)}), f32[16,48,128]{2,1,0:T(8,128)S(1)}, u32[]{:S(2)}, u32[]{:S(2)}) async-start(f32[16,48,128]{2,1,0:T(8,128)} %bitcast.1), calls=%async_computation | async-start | bytes 786432 | tf_op jit(solution)/shard_map/all_to_all | solution.py:322
  26.9 0.0 collective-permute-done.3.got_ref
  26.9 0.2 sum.3
  27.1 1.4 %collective-permute-start.4 = (f32[512,128]{1,0:T(8,128)S(1)}, f32[512,128]{1,0:T(8,128)S(1)}, u32[]{:S(2)}, u32[]{:S(2)}) collective-permute-start(f32[512,128]{1,0:T(8,128)S(1)} %sum.3), channel_id=1, source_target_pairs={{0,8},{2,10},{4,12},{6,14},{8,16},{10,18},{12,20},{14,22},{16,24},... | collective-permute-start | bytes 786440 | tf_op jit(solution)/shard_map/ppermute | solution.py:319
  28.5 0.0 collective-permute-done.5.got_ref
  28.5 0.2 sum.4
  28.6 0.8 %collective-permute-start.6 = (f32[512,128]{1,0:T(8,128)S(1)}, f32[512,128]{1,0:T(8,128)S(1)}, u32[]{:S(2)}, u32[]{:S(2)}) collective-permute-start(f32[512,128]{1,0:T(8,128)S(1)} %sum.4), channel_id=1, source_target_pairs={{0,24},{2,26},{4,28},{6,30},{8,0},{10,2},{12,4},{14,6},{16,8},{18,... | collective-permute-start | bytes 786440 | tf_op jit(solution)/shard_map/ppermute | solution.py:319
  29.5 0.0 collective-permute-done.7.got_ref
  29.5 0.1 sum.5.refs_2_
  29.6 4.6 %collective-permute-done.4.refs_0_ = f32[512,128]{1,0:T(8,128)S(1)} collective-permute-done((f32[512,128]{1,0:T(8,128)S(1)}, f32[512,128]{1,0:T(8,128)S(1)}, u32[]{:S(2)}, u32[]{:S(2)}) %collective-permute-start.4) | collective-permute-done | bytes 262176 | tf_op jit(solution)/shard_map/ppermute | solution.py:319
  34.2 1.3 %collective-permute-done.6.refs_1_ = f32[512,128]{1,0:T(8,128)S(1)} collective-permute-done((f32[512,128]{1,0:T(8,128)S(1)}, f32[512,128]{1,0:T(8,128)S(1)}, u32[]{:S(2)}, u32[]{:S(2)}) %collective-permute-start.6) | collective-permute-done | bytes 262176 | tf_op jit(solution)/shard_map/ppermute | solution.py:319
  35.4 0.9 %gather.1 = f32[1280,128]{1,0:T(8,128)} custom-call(f32[512,128]{1,0:T(8,128)S(1)} %collective-permute-done.4.refs_0_, f32[512,128]{1,0:T(8,128)S(1)} %collective-permute-done.6.refs_1_, f32[256,128]{1,0:T(8,128)S(1)} %sum.5.refs_2_), custom_call_target="tpu_custom_call" | custom-call | flops 1000 | bytes 1000 | tf_op jit(solution)/shard_map/gather/pallas_call | solution.py:351
  36.3 2.5 %all-to-all-done = f32[16,48,128]{2,1,0:T(8,128)S(1)} async-done(((f32[16,48,128]{2,1,0:T(8,128)}), f32[16,48,128]{2,1,0:T(8,128)S(1)}, u32[]{:S(2)}, u32[]{:S(2)}) %all-to-all-start) | async-done | bytes 393248 | tf_op jit(solution)/shard_map/all_to_all | solution.py:322
  38.8 6.9 %all-to-all-start.1 = ((f32[16,80,128]{2,1,0:T(8,128)}), f32[16,80,128]{2,1,0:T(8,128)S(1)}, u32[]{:S(2)}, u32[]{:S(2)}) async-start(f32[16,80,128]{2,1,0:T(8,128)} %bitcast.3), calls=%async_computation.1 | async-start | bytes 1310720 | tf_op jit(solution)/shard_map/all_to_all | solution.py:322
  45.7 0.7 %collective-permute-start.2 = (f32[512,128]{1,0:T(8,128)S(1)}, f32[512,128]{1,0:T(8,128)S(1)}, u32[]{:S(2)}, u32[]{:S(2)}) collective-permute-start(f32[512,128]{1,0:T(8,128)S(1)} %get-tuple-element.27), channel_id=1, source_target_pairs={{0,16},{2,18},{4,20},{6,22},{8,24},{10,26},{12,28},{14,30},{16,0},... | collective-permute-start | bytes 786440 | tf_op jit(solution)/shard_map/ppermute | solution.py:319
  46.4 7.2 %collective-permute-done.2.refs_0_ = f32[512,128]{1,0:T(8,128)S(1)} collective-permute-done((f32[512,128]{1,0:T(8,128)S(1)}, f32[512,128]{1,0:T(8,128)S(1)}, u32[]{:S(2)}, u32[]{:S(2)}) %collective-permute-start.2) | collective-permute-done | bytes 262176 | tf_op jit(solution)/shard_map/ppermute | solution.py:319
  53.6 8.5 %all-to-all-done.1 = f32[16,80,128]{2,1,0:T(8,128)S(1)} async-done(((f32[16,80,128]{2,1,0:T(8,128)}), f32[16,80,128]{2,1,0:T(8,128)S(1)}, u32[]{:S(2)}, u32[]{:S(2)}) %all-to-all-start.1) | async-done | bytes 655392 | tf_op jit(solution)/shard_map/all_to_all | solution.py:322
  62.1 1.1 %merge.1 = f32[2048,128]{1,0:T(8,128)} custom-call(f32[512,128]{1,0:T(8,128)S(1)} %collective-permute-done.2.refs_0_, f32[256,128]{1,0:T(8,128)S(1)} %get-tuple-element.28.refs_1_, f32[1280,128]{1,0:T(8,128)S(1)} %bitcast.10), custom_call_target="tpu_custom_call" | custom-call | flops 1000 | bytes 1000 | tf_op jit(solution)/shard_map/merge/pallas_call | solution.py:355
  (1 shorter events, 0.0 us)
Async XLA Ops:
  0.0 7.9 %collective-permute-start.1 = (f32[2,512,1024]{2,1,0:T(8,128)}, f32[2,512,1024]{2,1,0:T(8,128)S(1)}, u32[]{:S(2)}, u32[]{:S(2)}) collective-permute-start(f32[2,512,1024]{2,1,0:T(8,128)} %w_ref.1), channel_id=1, source_target_pairs={{0,1},{1,0},{2,3},{3,2},{4,5},{5,4},{6,7},{7,6},{8,9},{9,8},{10,11... | collective-permute-start | bytes 12582920 | tf_op jit(solution)/shard_map/ppermute | solution.py:278
  1.4 11.9 %collective-permute-start = (f32[96,1024]{1,0:T(8,128)S(1)}, f32[96,1024]{1,0:T(8,128)S(1)}, u32[]{:S(2)}, u32[]{:S(2)}) collective-permute-start(f32[96,1024]{1,0:T(8,128)S(1)} %first.1.after_ref), channel_id=1, source_target_pairs={{0,2},{2,0},{4,6},{6,4},{8,10},{10,8},{12,14},{14,12},{16,18},{18,... | collective-permute-start | bytes 1179656 | tf_op jit(solution)/shard_map/ppermute | solution.py:293
  10.3 16.6 %collective-permute-start.3 = (f32[64,1024]{1,0:T(8,128)S(1)}, f32[64,1024]{1,0:T(8,128)S(1)}, u32[]{:S(2)}, u32[]{:S(2)}) collective-permute-start(f32[64,1024]{1,0:T(8,128)S(1)} %get-tuple-element.29), channel_id=1, source_target_pairs={{0,2},{2,0},{4,6},{6,4},{8,10},{10,8},{12,14},{14,12},{16,18},{18,... | collective-permute-start | bytes 786440 | tf_op jit(solution)/shard_map/ppermute | solution.py:312
  11.3 17.2 %collective-permute-start.5 = (f32[64,1024]{1,0:T(8,128)S(1)}, f32[64,1024]{1,0:T(8,128)S(1)}, u32[]{:S(2)}, u32[]{:S(2)}) collective-permute-start(f32[64,1024]{1,0:T(8,128)S(1)} %get-tuple-element.31), channel_id=1, source_target_pairs={{0,2},{2,0},{4,6},{6,4},{8,10},{10,8},{12,14},{14,12},{16,18},{18,... | collective-permute-start | bytes 786440 | tf_op jit(solution)/shard_map/ppermute | solution.py:312
  12.4 17.0 %collective-permute-start.7 = (f32[32,1024]{1,0:T(8,128)S(1)}, f32[32,1024]{1,0:T(8,128)S(1)}, u32[]{:S(2)}, u32[]{:S(2)}) collective-permute-start(f32[32,1024]{1,0:T(8,128)S(1)} %get-tuple-element.33), channel_id=1, source_target_pairs={{0,2},{2,0},{4,6},{6,4},{8,10},{10,8},{12,14},{14,12},{16,18},{18,... | collective-permute-start | bytes 393224 | tf_op jit(solution)/shard_map/ppermute | solution.py:312
  15.1 23.7 %all-to-all-start = ((f32[16,48,128]{2,1,0:T(8,128)}), f32[16,48,128]{2,1,0:T(8,128)S(1)}, u32[]{:S(2)}, u32[]{:S(2)}) async-start(f32[16,48,128]{2,1,0:T(8,128)} %bitcast.1), calls=%async_computation | async-start | bytes 786432 | tf_op jit(solution)/shard_map/all_to_all | solution.py:322
  27.1 7.0 %collective-permute-start.4 = (f32[512,128]{1,0:T(8,128)S(1)}, f32[512,128]{1,0:T(8,128)S(1)}, u32[]{:S(2)}, u32[]{:S(2)}) collective-permute-start(f32[512,128]{1,0:T(8,128)S(1)} %sum.3), channel_id=1, source_target_pairs={{0,8},{2,10},{4,12},{6,14},{8,16},{10,18},{12,20},{14,22},{16,24},... | collective-permute-start | bytes 786440 | tf_op jit(solution)/shard_map/ppermute | solution.py:319
  28.6 6.8 %collective-permute-start.6 = (f32[512,128]{1,0:T(8,128)S(1)}, f32[512,128]{1,0:T(8,128)S(1)}, u32[]{:S(2)}, u32[]{:S(2)}) collective-permute-start(f32[512,128]{1,0:T(8,128)S(1)} %sum.4), channel_id=1, source_target_pairs={{0,24},{2,26},{4,28},{6,30},{8,0},{10,2},{12,4},{14,6},{16,8},{18,... | collective-permute-start | bytes 786440 | tf_op jit(solution)/shard_map/ppermute | solution.py:319
  38.8 23.3 %all-to-all-start.1 = ((f32[16,80,128]{2,1,0:T(8,128)}), f32[16,80,128]{2,1,0:T(8,128)S(1)}, u32[]{:S(2)}, u32[]{:S(2)}) async-start(f32[16,80,128]{2,1,0:T(8,128)} %bitcast.3), calls=%async_computation.1 | async-start | bytes 1310720 | tf_op jit(solution)/shard_map/all_to_all | solution.py:322
  45.7 8.0 %collective-permute-start.2 = (f32[512,128]{1,0:T(8,128)S(1)}, f32[512,128]{1,0:T(8,128)S(1)}, u32[]{:S(2)}, u32[]{:S(2)}) collective-permute-start(f32[512,128]{1,0:T(8,128)S(1)} %get-tuple-element.27), channel_id=1, source_target_pairs={{0,16},{2,18},{4,20},{6,22},{8,24},{10,26},{12,28},{14,30},{16,0},... | collective-permute-start | bytes 786440 | tf_op jit(solution)/shard_map/ppermute | solution.py:319

commit v6 on v5

--- a/solution.py
+++ b/solution.py
@@ -13,8 +13,8 @@
 Z = 8
 R = 4
 ALL = (0, 1, 2, 3)
-FIRST = ((2, ALL), (0, (0, 1)))
-SECOND = ((1, ALL), (3, ALL), (0, (2, 3)))
+FIRST = ((2, ALL), (0, (0,)))
+SECOND = ((1, ALL), (3, ALL), (0, (1, 2, 3)))
 PARTS = 4
 ADD_FLOPS = 10**11
 START_Z = 5

time: 64.2 us -> 64.2 us (level)
  starting transfers between devices: 26.2 us -> 27.1 us
    all_to_all x2, starting transfers between devices: 18.7 us -> 19.7 us  [across(): lax.all_to_all(block.reshape(2 * Z, -1, LANES), 'pair', split_axis=0, con...]
    all_to_all x2, waiting for transfers between devices: 10.9 us -> 10.2 us  [across(): lax.all_to_all(block.reshape(2 * Z, -1, LANES), 'pair', split_axis=0, con...]
  transfers between devices with their start and end apart: 10 -> 10, of which waited for: 5 -> 5; matrix products, arithmetic and copies ran while one was open for 0% -> 0% of each run, Pallas kernels for 19% -> 18%
where the time goes in v6:
time: 64.2 us; the launch traced here: 63.4 us
  starting transfers between devices  27.1 us (42%)
  waiting for transfers between devices  23.4 us (36%)
  Pallas kernels  12.8 us (20%)
    all_to_all x2, starting transfers between devices, across(): lax.all_to_all(block.reshape(2 * Z, -1, LANES), 'pair', split_axis=0, con...  19.7 us
    ppermute x3, waiting for transfers between devices, along_y(): return lax.ppermute(value, 'pair', perm)  13.2 us
    all_to_all x2, waiting for transfers between devices, across(): lax.all_to_all(block.reshape(2 * Z, -1, LANES), 'pair', split_axis=0, con...  10.2 us
    pallas_call x1, Pallas kernels, on_device(): call(near_kernel, 'near', [of(n_rest, width), of(n_rest, columns)] + halv...  4.95 us
    ppermute x3, starting transfers between devices, on_device(): got = [lax.ppermute(send, 'pair', swap) for send in sends]  2.96 us
    ppermute x3, starting transfers between devices, along_y(): return lax.ppermute(value, 'pair', perm)  2.9 us
    pallas_call x1, Pallas kernels, on_device(): call(far_kernel, 'far', [of(n, columns) for n in [count(FIRST)] + sizes +...  2.42 us
    pallas_call x1, Pallas kernels, on_device(): call(last_kernel, 'last', of(count(FIRST) * tiles, LANES), [vmem()] * 6)  1.59 us
  transfers between devices with their start and end apart: 10, of which 5 were waited for; matrix products, arithmetic and copies ran while one was open for 0% of the time, Pallas kernels for 18%

profile of v6, /device:TPU:16, one launch (start us, length us, event | category | flops | bytes accessed | tf_op | source)
XLA Modules:
  0.0 63.4 jit_solution(17553150424157683427)
XLA Ops:
  0.0 0.0 collective-permute-start.1
  0.0 1.4 %first.1.after_ref = f32[80,1024]{1,0:T(8,128)S(1)} custom-call(f32[8,4,16,1024]{3,2,1,0:T(8,128)} %bitcast.12, s32[1,8,16]{2,1,0:T(8,128)} %mask_ref.3), custom_call_target="tpu_custom_call" | custom-call | flops 1000 | bytes 1000 | tf_op jit(solution)/shard_map/first/pallas_call | solution.py:282
  1.4 1.6 %collective-permute-start = (f32[80,1024]{1,0:T(8,128)S(1)}, f32[80,1024]{1,0:T(8,128)S(1)}, u32[]{:S(2)}, u32[]{:S(2)}) collective-permute-start(f32[80,1024]{1,0:T(8,128)S(1)} %first.1.after_ref), channel_id=1, source_target_pairs={{0,2},{2,0},{4,6},{6,4},{8,10},{10,8},{12,14},{14,12},{16,18},{18,... | collective-permute-start | bytes 983048 | tf_op jit(solution)/shard_map/ppermute | solution.py:293
  3.0 5.0 %near.1 = (f32[432,1024]{1,0:T(8,128)S(1)}, f32[432,1024]{1,0:T(8,128)S(1)}, bf16[512,1024]{1,0:T(8,128)(2,1)S(1)}, bf16[512,1024]{1,0:T(8,128)(2,1)S(1)}) custom-call(f32[1,512,1024]{2,1,0:T(8,128)} %t_ref.1, s32[1,8,16]{2,1,0:T(8,128)} %mask_ref.3, f32[2,512,1024]{2,1,0:T(8,128)} %w_ref.1, f32[80,1024]{1,0:T(8,128)S(1)} %first.1.after_ref), custom_call_target="tpu_custom_call" | custom-call | flops 1000 | bytes 1000 | tf_op jit(solution)/shard_map/near/pallas_call | solution.py:296
  8.0 0.0 collective-permute-done.1.w_ref
  8.0 2.4 %far.1 = (f32[80,1024]{1,0:T(8,128)S(1)}, f32[64,1024]{1,0:T(8,128)S(1)}, f32[64,1024]{1,0:T(8,128)S(1)}, f32[48,1024]{1,0:T(8,128)S(1)}, f32[64,1024]{1,0:T(8,1...) custom-call(f32[432,1024]{1,0:T(8,128)S(1)} %get-tuple-element.22.x_, ...), custom_call_target="tpu_custom_call" | custom-call | flops 1000 | bytes 1000 | tf_op jit(solution)/shard_map/far/pallas_call | solution.py:304
  10.4 0.9 %collective-permute-start.3 = (f32[64,1024]{1,0:T(8,128)S(1)}, f32[64,1024]{1,0:T(8,128)S(1)}, u32[]{:S(2)}, u32[]{:S(2)}) collective-permute-start(f32[64,1024]{1,0:T(8,128)S(1)} %get-tuple-element.29), channel_id=1, source_target_pairs={{0,2},{2,0},{4,6},{6,4},{8,10},{10,8},{12,14},{14,12},{16,18},{18,... | collective-permute-start | bytes 786440 | tf_op jit(solution)/shard_map/ppermute | solution.py:312
  11.3 1.2 %collective-permute-start.5 = (f32[64,1024]{1,0:T(8,128)S(1)}, f32[64,1024]{1,0:T(8,128)S(1)}, u32[]{:S(2)}, u32[]{:S(2)}) collective-permute-start(f32[64,1024]{1,0:T(8,128)S(1)} %get-tuple-element.31), channel_id=1, source_target_pairs={{0,2},{2,0},{4,6},{6,4},{8,10},{10,8},{12,14},{14,12},{16,18},{18,... | collective-permute-start | bytes 786440 | tf_op jit(solution)/shard_map/ppermute | solution.py:312
  12.5 0.8 %collective-permute-start.7 = (f32[48,1024]{1,0:T(8,128)S(1)}, f32[48,1024]{1,0:T(8,128)S(1)}, u32[]{:S(2)}, u32[]{:S(2)}) collective-permute-start(f32[48,1024]{1,0:T(8,128)S(1)} %get-tuple-element.33), channel_id=1, source_target_pairs={{0,2},{2,0},{4,6},{6,4},{8,10},{10,8},{12,14},{14,12},{16,18},{18,... | collective-permute-start | bytes 589832 | tf_op jit(solution)/shard_map/ppermute | solution.py:312
  13.4 0.0 collective-permute-done.got_ref
  13.4 1.6 %last.1 = f32[640,128]{1,0:T(8,128)} custom-call(f32[80,1024]{1,0:T(8,128)S(1)} %collective-permute-done.got_ref, bf16[512,1024]{1,0:T(8,128)(2,1)S(1)} %get-tuple-element.20.high0_ref, bf16[512,1024]{1,0:T(8,128)(2,1)S(1)} %get-tuple-element.21.low0_ref, bf16[512,1024]{1,0:T(8,128)(2,1)S(1)} %get-tuple-element.24.high1_ref, ...), custom_call_target="tpu_custom_call" | custom-call | flops 1000 | bytes 1000 | tf_op jit(solution)/shard_map/last/pallas_call | solution.py:336
  15.0 11.4 %all-to-all-start = ((f32[16,40,128]{2,1,0:T(8,128)}), f32[16,40,128]{2,1,0:T(8,128)S(1)}, u32[]{:S(2)}, u32[]{:S(2)}) async-start(f32[16,40,128]{2,1,0:T(8,128)} %bitcast.1), calls=%async_computation | async-start | bytes 655360 | tf_op jit(solution)/shard_map/all_to_all | solution.py:322
  26.4 0.0 collective-permute-done.3.got_ref
  26.4 0.2 sum.3
  26.6 1.4 %collective-permute-start.4 = (f32[512,128]{1,0:T(8,128)S(1)}, f32[512,128]{1,0:T(8,128)S(1)}, u32[]{:S(2)}, u32[]{:S(2)}) collective-permute-start(f32[512,128]{1,0:T(8,128)S(1)} %sum.3), channel_id=1, source_target_pairs={{0,8},{2,10},{4,12},{6,14},{8,16},{10,18},{12,20},{14,22},{16,24},... | collective-permute-start | bytes 786440 | tf_op jit(solution)/shard_map/ppermute | solution.py:319
  27.9 0.0 collective-permute-done.5.got_ref
  27.9 0.2 sum.4
  28.1 0.8 %collective-permute-start.6 = (f32[512,128]{1,0:T(8,128)S(1)}, f32[512,128]{1,0:T(8,128)S(1)}, u32[]{:S(2)}, u32[]{:S(2)}) collective-permute-start(f32[512,128]{1,0:T(8,128)S(1)} %sum.4), channel_id=1, source_target_pairs={{0,24},{2,26},{4,28},{6,30},{8,0},{10,2},{12,4},{14,6},{16,8},{18,... | collective-permute-start | bytes 786440 | tf_op jit(solution)/shard_map/ppermute | solution.py:319
  28.9 0.0 collective-permute-done.7.got_ref
  28.9 0.1 sum.5.refs_2_
  29.0 4.7 %collective-permute-done.4.refs_0_ = f32[512,128]{1,0:T(8,128)S(1)} collective-permute-done((f32[512,128]{1,0:T(8,128)S(1)}, f32[512,128]{1,0:T(8,128)S(1)}, u32[]{:S(2)}, u32[]{:S(2)}) %collective-permute-start.4) | collective-permute-done | bytes 262176 | tf_op jit(solution)/shard_map/ppermute | solution.py:319
  33.6 1.3 %collective-permute-done.6.refs_1_ = f32[512,128]{1,0:T(8,128)S(1)} collective-permute-done((f32[512,128]{1,0:T(8,128)S(1)}, f32[512,128]{1,0:T(8,128)S(1)}, u32[]{:S(2)}, u32[]{:S(2)}) %collective-permute-start.6) | collective-permute-done | bytes 262176 | tf_op jit(solution)/shard_map/ppermute | solution.py:319
  34.9 0.9 %gather.1 = f32[1408,128]{1,0:T(8,128)} custom-call(f32[512,128]{1,0:T(8,128)S(1)} %collective-permute-done.4.refs_0_, f32[512,128]{1,0:T(8,128)S(1)} %collective-permute-done.6.refs_1_, f32[384,128]{1,0:T(8,128)S(1)} %sum.5.refs_2_), custom_call_target="tpu_custom_call" | custom-call | flops 1000 | bytes 1000 | tf_op jit(solution)/shard_map/gather/pallas_call | solution.py:351
  35.8 1.1 %all-to-all-done = f32[16,40,128]{2,1,0:T(8,128)S(1)} async-done(((f32[16,40,128]{2,1,0:T(8,128)}), f32[16,40,128]{2,1,0:T(8,128)S(1)}, u32[]{:S(2)}, u32[]{:S(2)}) %all-to-all-start) | async-done | bytes 327712 | tf_op jit(solution)/shard_map/all_to_all | solution.py:322
  36.9 8.3 %all-to-all-start.1 = ((f32[16,88,128]{2,1,0:T(8,128)}), f32[16,88,128]{2,1,0:T(8,128)S(1)}, u32[]{:S(2)}, u32[]{:S(2)}) async-start(f32[16,88,128]{2,1,0:T(8,128)} %bitcast.3), calls=%async_computation.1 | async-start | bytes 1441792 | tf_op jit(solution)/shard_map/all_to_all | solution.py:322
  45.2 0.7 %collective-permute-start.2 = (f32[512,128]{1,0:T(8,128)S(1)}, f32[512,128]{1,0:T(8,128)S(1)}, u32[]{:S(2)}, u32[]{:S(2)}) collective-permute-start(f32[512,128]{1,0:T(8,128)S(1)} %get-tuple-element.27), channel_id=1, source_target_pairs={{0,16},{2,18},{4,20},{6,22},{8,24},{10,26},{12,28},{14,30},{16,0},... | collective-permute-start | bytes 786440 | tf_op jit(solution)/shard_map/ppermute | solution.py:319
  45.9 7.2 %collective-permute-done.2.refs_0_ = f32[512,128]{1,0:T(8,128)S(1)} collective-permute-done((f32[512,128]{1,0:T(8,128)S(1)}, f32[512,128]{1,0:T(8,128)S(1)}, u32[]{:S(2)}, u32[]{:S(2)}) %collective-permute-start.2) | collective-permute-done | bytes 262176 | tf_op jit(solution)/shard_map/ppermute | solution.py:319
  53.1 9.2 %all-to-all-done.1 = f32[16,88,128]{2,1,0:T(8,128)S(1)} async-done(((f32[16,88,128]{2,1,0:T(8,128)}), f32[16,88,128]{2,1,0:T(8,128)S(1)}, u32[]{:S(2)}, u32[]{:S(2)}) %all-to-all-start.1) | async-done | bytes 720928 | tf_op jit(solution)/shard_map/all_to_all | solution.py:322
  62.3 1.1 %merge.1 = f32[2048,128]{1,0:T(8,128)} custom-call(f32[512,128]{1,0:T(8,128)S(1)} %collective-permute-done.2.refs_0_, f32[128,128]{1,0:T(8,128)S(1)} %get-tuple-element.28.refs_1_, f32[1408,128]{1,0:T(8,128)S(1)} %bitcast.10), custom_call_target="tpu_custom_call" | custom-call | flops 1000 | bytes 1000 | tf_op jit(solution)/shard_map/merge/pallas_call | solution.py:355
  (1 shorter events, 0.0 us)
Async XLA Ops:
  0.0 8.0 %collective-permute-start.1 = (f32[2,512,1024]{2,1,0:T(8,128)}, f32[2,512,1024]{2,1,0:T(8,128)S(1)}, u32[]{:S(2)}, u32[]{:S(2)}) collective-permute-start(f32[2,512,1024]{2,1,0:T(8,128)} %w_ref.1), channel_id=1, source_target_pairs={{0,1},{1,0},{2,3},{3,2},{4,5},{5,4},{6,7},{7,6},{8,9},{9,8},{10,11... | collective-permute-start | bytes 12582920 | tf_op jit(solution)/shard_map/ppermute | solution.py:278
  1.4 11.9 %collective-permute-start = (f32[80,1024]{1,0:T(8,128)S(1)}, f32[80,1024]{1,0:T(8,128)S(1)}, u32[]{:S(2)}, u32[]{:S(2)}) collective-permute-start(f32[80,1024]{1,0:T(8,128)S(1)} %first.1.after_ref), channel_id=1, source_target_pairs={{0,2},{2,0},{4,6},{6,4},{8,10},{10,8},{12,14},{14,12},{16,18},{18,... | collective-permute-start | bytes 983048 | tf_op jit(solution)/shard_map/ppermute | solution.py:293
  10.4 16.0 %collective-permute-start.3 = (f32[64,1024]{1,0:T(8,128)S(1)}, f32[64,1024]{1,0:T(8,128)S(1)}, u32[]{:S(2)}, u32[]{:S(2)}) collective-permute-start(f32[64,1024]{1,0:T(8,128)S(1)} %get-tuple-element.29), channel_id=1, source_target_pairs={{0,2},{2,0},{4,6},{6,4},{8,10},{10,8},{12,14},{14,12},{16,18},{18,... | collective-permute-start | bytes 786440 | tf_op jit(solution)/shard_map/ppermute | solution.py:312
  11.3 16.6 %collective-permute-start.5 = (f32[64,1024]{1,0:T(8,128)S(1)}, f32[64,1024]{1,0:T(8,128)S(1)}, u32[]{:S(2)}, u32[]{:S(2)}) collective-permute-start(f32[64,1024]{1,0:T(8,128)S(1)} %get-tuple-element.31), channel_id=1, source_target_pairs={{0,2},{2,0},{4,6},{6,4},{8,10},{10,8},{12,14},{14,12},{16,18},{18,... | collective-permute-start | bytes 786440 | tf_op jit(solution)/shard_map/ppermute | solution.py:312
  12.5 16.4 %collective-permute-start.7 = (f32[48,1024]{1,0:T(8,128)S(1)}, f32[48,1024]{1,0:T(8,128)S(1)}, u32[]{:S(2)}, u32[]{:S(2)}) collective-permute-start(f32[48,1024]{1,0:T(8,128)S(1)} %get-tuple-element.33), channel_id=1, source_target_pairs={{0,2},{2,0},{4,6},{6,4},{8,10},{10,8},{12,14},{14,12},{16,18},{18,... | collective-permute-start | bytes 589832 | tf_op jit(solution)/shard_map/ppermute | solution.py:312
  15.0 21.9 %all-to-all-start = ((f32[16,40,128]{2,1,0:T(8,128)}), f32[16,40,128]{2,1,0:T(8,128)S(1)}, u32[]{:S(2)}, u32[]{:S(2)}) async-start(f32[16,40,128]{2,1,0:T(8,128)} %bitcast.1), calls=%async_computation | async-start | bytes 655360 | tf_op jit(solution)/shard_map/all_to_all | solution.py:322
  26.6 7.1 %collective-permute-start.4 = (f32[512,128]{1,0:T(8,128)S(1)}, f32[512,128]{1,0:T(8,128)S(1)}, u32[]{:S(2)}, u32[]{:S(2)}) collective-permute-start(f32[512,128]{1,0:T(8,128)S(1)} %sum.3), channel_id=1, source_target_pairs={{0,8},{2,10},{4,12},{6,14},{8,16},{10,18},{12,20},{14,22},{16,24},... | collective-permute-start | bytes 786440 | tf_op jit(solution)/shard_map/ppermute | solution.py:319
  28.1 6.8 %collective-permute-start.6 = (f32[512,128]{1,0:T(8,128)S(1)}, f32[512,128]{1,0:T(8,128)S(1)}, u32[]{:S(2)}, u32[]{:S(2)}) collective-permute-start(f32[512,128]{1,0:T(8,128)S(1)} %sum.4), channel_id=1, source_target_pairs={{0,24},{2,26},{4,28},{6,30},{8,0},{10,2},{12,4},{14,6},{16,8},{18,... | collective-permute-start | bytes 786440 | tf_op jit(solution)/shard_map/ppermute | solution.py:319
  36.9 25.5 %all-to-all-start.1 = ((f32[16,88,128]{2,1,0:T(8,128)}), f32[16,88,128]{2,1,0:T(8,128)S(1)}, u32[]{:S(2)}, u32[]{:S(2)}) async-start(f32[16,88,128]{2,1,0:T(8,128)} %bitcast.3), calls=%async_computation.1 | async-start | bytes 1441792 | tf_op jit(solution)/shard_map/all_to_all | solution.py:322
  45.2 8.0 %collective-permute-start.2 = (f32[512,128]{1,0:T(8,128)S(1)}, f32[512,128]{1,0:T(8,128)S(1)}, u32[]{:S(2)}, u32[]{:S(2)}) collective-permute-start(f32[512,128]{1,0:T(8,128)S(1)} %get-tuple-element.27), channel_id=1, source_target_pairs={{0,16},{2,18},{4,20},{6,22},{8,24},{10,26},{12,28},{14,30},{16,0},... | collective-permute-start | bytes 786440 | tf_op jit(solution)/shard_map/ppermute | solution.py:319

commit v7 on v5

--- a/solution.py
+++ b/solution.py
@@ -14,7 +14,7 @@
 R = 4
 ALL = (0, 1, 2, 3)
 FIRST = ((2, ALL), (0, (0, 1)))
-SECOND = ((1, ALL), (3, ALL), (0, (2, 3)))
+SECOND = ((3, ALL), (1, ALL), (0, (2, 3)))
 PARTS = 4
 ADD_FLOPS = 10**11
 START_Z = 5

time: 64.2 us -> 64.3 us (level)
  starting transfers between devices: 26.2 us -> 28.8 us
  waiting for transfers between devices: 24 us -> 21.4 us
    ppermute x3, waiting for transfers between devices: 13.1 us -> 9.38 us  [along_y(): return lax.ppermute(value, 'pair', perm)]
    ppermute x3, starting transfers between devices: 2.9 us -> 6.08 us  [along_y(): return lax.ppermute(value, 'pair', perm)]
    all_to_all x2, waiting for transfers between devices: 10.9 us -> 12 us  [across(): lax.all_to_all(block.reshape(2 * Z, -1, LANES), 'pair', split_axis=0, con...]
where the time goes in v7:
time: 64.3 us; the launch traced here: 63.1 us
  starting transfers between devices  28.8 us (45%)
  waiting for transfers between devices  21.4 us (33%)
  Pallas kernels  12.8 us (20%)
    all_to_all x2, starting transfers between devices, across(): lax.all_to_all(block.reshape(2 * Z, -1, LANES), 'pair', split_axis=0, con...  18.1 us
    all_to_all x2, waiting for transfers between devices, across(): lax.all_to_all(block.reshape(2 * Z, -1, LANES), 'pair', split_axis=0, con...  12 us
    ppermute x3, waiting for transfers between devices, along_y(): return lax.ppermute(value, 'pair', perm)  9.38 us
    ppermute x3, starting transfers between devices, along_y(): return lax.ppermute(value, 'pair', perm)  6.08 us
    pallas_call x1, Pallas kernels, on_device(): call(near_kernel, 'near', [of(n_rest, width), of(n_rest, columns)] + halv...  4.9 us
    ppermute x3, starting transfers between devices, on_device(): got = [lax.ppermute(send, 'pair', swap) for send in sends]  3.01 us
    pallas_call x1, Pallas kernels, on_device(): call(far_kernel, 'far', [of(n, columns) for n in [count(FIRST)] + sizes +...  2.36 us
    pallas_call x1, Pallas kernels, on_device(): call(last_kernel, 'last', of(count(FIRST) * tiles, LANES), [vmem()] * 6)  1.79 us
  transfers between devices with their start and end apart: 10, of which 5 were waited for; matrix products, arithmetic and copies ran while one was open for 0% of the time, Pallas kernels for 19%

profile of v7, /device:TPU:16, one launch (start us, length us, event | category | flops | bytes accessed | tf_op | source)
XLA Modules:
  0.0 63.1 jit_solution(1928847120759655601)
XLA Ops:
  0.0 0.0 collective-permute-start.1
  0.0 1.4 %first.1.after_ref = f32[96,1024]{1,0:T(8,128)S(1)} custom-call(f32[8,4,16,1024]{3,2,1,0:T(8,128)} %bitcast.12, s32[1,8,16]{2,1,0:T(8,128)} %mask_ref.3), custom_call_target="tpu_custom_call" | custom-call | flops 1000 | bytes 1000 | tf_op jit(solution)/shard_map/first/pallas_call | solution.py:282
  1.4 1.6 %collective-permute-start = (f32[96,1024]{1,0:T(8,128)S(1)}, f32[96,1024]{1,0:T(8,128)S(1)}, u32[]{:S(2)}, u32[]{:S(2)}) collective-permute-start(f32[96,1024]{1,0:T(8,128)S(1)} %first.1.after_ref), channel_id=1, source_target_pairs={{0,2},{2,0},{4,6},{6,4},{8,10},{10,8},{12,14},{14,12},{16,18},{18,... | collective-permute-start | bytes 1179656 | tf_op jit(solution)/shard_map/ppermute | solution.py:293
  3.0 4.9 %near.1 = (f32[416,1024]{1,0:T(8,128)S(1)}, f32[416,1024]{1,0:T(8,128)S(1)}, bf16[512,1024]{1,0:T(8,128)(2,1)S(1)}, bf16[512,1024]{1,0:T(8,128)(2,1)S(1)}) custom-call(f32[1,512,1024]{2,1,0:T(8,128)} %t_ref.1, s32[1,8,16]{2,1,0:T(8,128)} %mask_ref.3, f32[2,512,1024]{2,1,0:T(8,128)} %w_ref.1, f32[96,1024]{1,0:T(8,128)S(1)} %first.1.after_ref), custom_call_target="tpu_custom_call" | custom-call | flops 1000 | bytes 1000 | tf_op jit(solution)/shard_map/near/pallas_call | solution.py:296
  7.9 0.0 collective-permute-done.1.w_ref
  7.9 2.4 %far.1 = (f32[96,1024]{1,0:T(8,128)S(1)}, f32[64,1024]{1,0:T(8,128)S(1)}, f32[64,1024]{1,0:T(8,128)S(1)}, f32[32,1024]{1,0:T(8,128)S(1)}, f32[64,1024]{1,0:T(8,1...) custom-call(f32[416,1024]{1,0:T(8,128)S(1)} %get-tuple-element.22.x_, ...), custom_call_target="tpu_custom_call" | custom-call | flops 1000 | bytes 1000 | tf_op jit(solution)/shard_map/far/pallas_call | solution.py:304
  10.3 1.0 %collective-permute-start.3 = (f32[64,1024]{1,0:T(8,128)S(1)}, f32[64,1024]{1,0:T(8,128)S(1)}, u32[]{:S(2)}, u32[]{:S(2)}) collective-permute-start(f32[64,1024]{1,0:T(8,128)S(1)} %get-tuple-element.29), channel_id=1, source_target_pairs={{0,2},{2,0},{4,6},{6,4},{8,10},{10,8},{12,14},{14,12},{16,18},{18,... | collective-permute-start | bytes 786440 | tf_op jit(solution)/shard_map/ppermute | solution.py:312
  11.3 1.1 %collective-permute-start.5 = (f32[64,1024]{1,0:T(8,128)S(1)}, f32[64,1024]{1,0:T(8,128)S(1)}, u32[]{:S(2)}, u32[]{:S(2)}) collective-permute-start(f32[64,1024]{1,0:T(8,128)S(1)} %get-tuple-element.31), channel_id=1, source_target_pairs={{0,2},{2,0},{4,6},{6,4},{8,10},{10,8},{12,14},{14,12},{16,18},{18,... | collective-permute-start | bytes 786440 | tf_op jit(solution)/shard_map/ppermute | solution.py:312
  12.4 0.9 %collective-permute-start.7 = (f32[32,1024]{1,0:T(8,128)S(1)}, f32[32,1024]{1,0:T(8,128)S(1)}, u32[]{:S(2)}, u32[]{:S(2)}) collective-permute-start(f32[32,1024]{1,0:T(8,128)S(1)} %get-tuple-element.33), channel_id=1, source_target_pairs={{0,2},{2,0},{4,6},{6,4},{8,10},{10,8},{12,14},{14,12},{16,18},{18,... | collective-permute-start | bytes 393224 | tf_op jit(solution)/shard_map/ppermute | solution.py:312
  13.3 0.0 collective-permute-done.got_ref
  13.3 1.8 %last.1 = f32[768,128]{1,0:T(8,128)} custom-call(f32[96,1024]{1,0:T(8,128)S(1)} %collective-permute-done.got_ref, bf16[512,1024]{1,0:T(8,128)(2,1)S(1)} %get-tuple-element.20.high0_ref, bf16[512,1024]{1,0:T(8,128)(2,1)S(1)} %get-tuple-element.21.low0_ref, bf16[512,1024]{1,0:T(8,128)(2,1)S(1)} %get-tuple-element.24.high1_ref, ...), custom_call_target="tpu_custom_call" | custom-call | flops 1000 | bytes 1000 | tf_op jit(solution)/shard_map/last/pallas_call | solution.py:336
  15.1 11.8 %all-to-all-start = ((f32[16,48,128]{2,1,0:T(8,128)}), f32[16,48,128]{2,1,0:T(8,128)S(1)}, u32[]{:S(2)}, u32[]{:S(2)}) async-start(f32[16,48,128]{2,1,0:T(8,128)} %bitcast.1), calls=%async_computation | async-start | bytes 786432 | tf_op jit(solution)/shard_map/all_to_all | solution.py:322
  26.9 0.0 collective-permute-done.3.got_ref
  26.9 0.2 sum.3
  27.1 0.5 collective-permute-start.4
  27.6 0.0 collective-permute-done.5.got_ref
  27.6 0.2 sum.4
  27.8 1.7 %collective-permute-start.6 = (f32[512,128]{1,0:T(8,128)S(1)}, f32[512,128]{1,0:T(8,128)S(1)}, u32[]{:S(2)}, u32[]{:S(2)}) collective-permute-start(f32[512,128]{1,0:T(8,128)S(1)} %sum.4), channel_id=1, source_target_pairs={{0,8},{2,10},{4,12},{6,14},{8,16},{10,18},{12,20},{14,22},{16,24},... | collective-permute-start | bytes 786440 | tf_op jit(solution)/shard_map/ppermute | solution.py:319
  29.5 0.0 collective-permute-done.7.got_ref
  29.5 0.1 sum.5.refs_2_
  29.6 4.6 %collective-permute-done.4.refs_0_ = f32[512,128]{1,0:T(8,128)S(1)} collective-permute-done((f32[512,128]{1,0:T(8,128)S(1)}, f32[512,128]{1,0:T(8,128)S(1)}, u32[]{:S(2)}, u32[]{:S(2)}) %collective-permute-start.4) | collective-permute-done | bytes 262176 | tf_op jit(solution)/shard_map/ppermute | solution.py:319
  34.2 0.4 collective-permute-done.6.refs_1_
  34.6 0.9 %gather.1 = f32[1280,128]{1,0:T(8,128)} custom-call(f32[512,128]{1,0:T(8,128)S(1)} %collective-permute-done.4.refs_0_, f32[512,128]{1,0:T(8,128)S(1)} %collective-permute-done.6.refs_1_, f32[256,128]{1,0:T(8,128)S(1)} %sum.5.refs_2_), custom_call_target="tpu_custom_call" | custom-call | flops 1000 | bytes 1000 | tf_op jit(solution)/shard_map/gather/pallas_call | solution.py:351
  35.5 3.3 %all-to-all-done = f32[16,48,128]{2,1,0:T(8,128)S(1)} async-done(((f32[16,48,128]{2,1,0:T(8,128)}), f32[16,48,128]{2,1,0:T(8,128)S(1)}, u32[]{:S(2)}, u32[]{:S(2)}) %all-to-all-start) | async-done | bytes 393248 | tf_op jit(solution)/shard_map/all_to_all | solution.py:322
  38.8 6.3 %all-to-all-start.1 = ((f32[16,80,128]{2,1,0:T(8,128)}), f32[16,80,128]{2,1,0:T(8,128)S(1)}, u32[]{:S(2)}, u32[]{:S(2)}) async-start(f32[16,80,128]{2,1,0:T(8,128)} %bitcast.3), calls=%async_computation.1 | async-start | bytes 1310720 | tf_op jit(solution)/shard_map/all_to_all | solution.py:322
  45.1 3.9 %collective-permute-start.2 = (f32[512,128]{1,0:T(8,128)S(1)}, f32[512,128]{1,0:T(8,128)S(1)}, u32[]{:S(2)}, u32[]{:S(2)}) collective-permute-start(f32[512,128]{1,0:T(8,128)S(1)} %get-tuple-element.27), channel_id=1, source_target_pairs={{0,16},{2,18},{4,20},{6,22},{8,24},{10,26},{12,28},{14,30},{16,0},... | collective-permute-start | bytes 786440 | tf_op jit(solution)/shard_map/ppermute | solution.py:319
  49.0 4.4 %collective-permute-done.2.refs_0_ = f32[512,128]{1,0:T(8,128)S(1)} collective-permute-done((f32[512,128]{1,0:T(8,128)S(1)}, f32[512,128]{1,0:T(8,128)S(1)}, u32[]{:S(2)}, u32[]{:S(2)}) %collective-permute-start.2) | collective-permute-done | bytes 262176 | tf_op jit(solution)/shard_map/ppermute | solution.py:319
  53.4 8.7 %all-to-all-done.1 = f32[16,80,128]{2,1,0:T(8,128)S(1)} async-done(((f32[16,80,128]{2,1,0:T(8,128)}), f32[16,80,128]{2,1,0:T(8,128)S(1)}, u32[]{:S(2)}, u32[]{:S(2)}) %all-to-all-start.1) | async-done | bytes 655392 | tf_op jit(solution)/shard_map/all_to_all | solution.py:322
  62.1 1.1 %merge.1 = f32[2048,128]{1,0:T(8,128)} custom-call(f32[512,128]{1,0:T(8,128)S(1)} %collective-permute-done.2.refs_0_, f32[256,128]{1,0:T(8,128)S(1)} %get-tuple-element.28.refs_1_, f32[1280,128]{1,0:T(8,128)S(1)} %bitcast.10), custom_call_target="tpu_custom_call" | custom-call | flops 1000 | bytes 1000 | tf_op jit(solution)/shard_map/merge/pallas_call | solution.py:355
  (1 shorter events, 0.0 us)
Async XLA Ops:
  0.0 7.9 %collective-permute-start.1 = (f32[2,512,1024]{2,1,0:T(8,128)}, f32[2,512,1024]{2,1,0:T(8,128)S(1)}, u32[]{:S(2)}, u32[]{:S(2)}) collective-permute-start(f32[2,512,1024]{2,1,0:T(8,128)} %w_ref.1), channel_id=1, source_target_pairs={{0,1},{1,0},{2,3},{3,2},{4,5},{5,4},{6,7},{7,6},{8,9},{9,8},{10,11... | collective-permute-start | bytes 12582920 | tf_op jit(solution)/shard_map/ppermute | solution.py:278
  1.4 11.9 %collective-permute-start = (f32[96,1024]{1,0:T(8,128)S(1)}, f32[96,1024]{1,0:T(8,128)S(1)}, u32[]{:S(2)}, u32[]{:S(2)}) collective-permute-start(f32[96,1024]{1,0:T(8,128)S(1)} %first.1.after_ref), channel_id=1, source_target_pairs={{0,2},{2,0},{4,6},{6,4},{8,10},{10,8},{12,14},{14,12},{16,18},{18,... | collective-permute-start | bytes 1179656 | tf_op jit(solution)/shard_map/ppermute | solution.py:293
  10.3 16.6 %collective-permute-start.3 = (f32[64,1024]{1,0:T(8,128)S(1)}, f32[64,1024]{1,0:T(8,128)S(1)}, u32[]{:S(2)}, u32[]{:S(2)}) collective-permute-start(f32[64,1024]{1,0:T(8,128)S(1)} %get-tuple-element.29), channel_id=1, source_target_pairs={{0,2},{2,0},{4,6},{6,4},{8,10},{10,8},{12,14},{14,12},{16,18},{18,... | collective-permute-start | bytes 786440 | tf_op jit(solution)/shard_map/ppermute | solution.py:312
  11.3 16.3 %collective-permute-start.5 = (f32[64,1024]{1,0:T(8,128)S(1)}, f32[64,1024]{1,0:T(8,128)S(1)}, u32[]{:S(2)}, u32[]{:S(2)}) collective-permute-start(f32[64,1024]{1,0:T(8,128)S(1)} %get-tuple-element.31), channel_id=1, source_target_pairs={{0,2},{2,0},{4,6},{6,4},{8,10},{10,8},{12,14},{14,12},{16,18},{18,... | collective-permute-start | bytes 786440 | tf_op jit(solution)/shard_map/ppermute | solution.py:312
  12.4 17.0 %collective-permute-start.7 = (f32[32,1024]{1,0:T(8,128)S(1)}, f32[32,1024]{1,0:T(8,128)S(1)}, u32[]{:S(2)}, u32[]{:S(2)}) collective-permute-start(f32[32,1024]{1,0:T(8,128)S(1)} %get-tuple-element.33), channel_id=1, source_target_pairs={{0,2},{2,0},{4,6},{6,4},{8,10},{10,8},{12,14},{14,12},{16,18},{18,... | collective-permute-start | bytes 393224 | tf_op jit(solution)/shard_map/ppermute | solution.py:312
  15.1 23.7 %all-to-all-start = ((f32[16,48,128]{2,1,0:T(8,128)}), f32[16,48,128]{2,1,0:T(8,128)S(1)}, u32[]{:S(2)}, u32[]{:S(2)}) async-start(f32[16,48,128]{2,1,0:T(8,128)} %bitcast.1), calls=%async_computation | async-start | bytes 786432 | tf_op jit(solution)/shard_map/all_to_all | solution.py:322
  27.1 7.0 %collective-permute-start.4 = (f32[512,128]{1,0:T(8,128)S(1)}, f32[512,128]{1,0:T(8,128)S(1)}, u32[]{:S(2)}, u32[]{:S(2)}) collective-permute-start(f32[512,128]{1,0:T(8,128)S(1)} %sum.3), channel_id=1, source_target_pairs={{0,24},{2,26},{4,28},{6,30},{8,0},{10,2},{12,4},{14,6},{16,8},{18,... | collective-permute-start | bytes 786440 | tf_op jit(solution)/shard_map/ppermute | solution.py:319
  27.8 6.8 %collective-permute-start.6 = (f32[512,128]{1,0:T(8,128)S(1)}, f32[512,128]{1,0:T(8,128)S(1)}, u32[]{:S(2)}, u32[]{:S(2)}) collective-permute-start(f32[512,128]{1,0:T(8,128)S(1)} %sum.4), channel_id=1, source_target_pairs={{0,8},{2,10},{4,12},{6,14},{8,16},{10,18},{12,20},{14,22},{16,24},... | collective-permute-start | bytes 786440 | tf_op jit(solution)/shard_map/ppermute | solution.py:319
  38.8 23.3 %all-to-all-start.1 = ((f32[16,80,128]{2,1,0:T(8,128)}), f32[16,80,128]{2,1,0:T(8,128)S(1)}, u32[]{:S(2)}, u32[]{:S(2)}) async-start(f32[16,80,128]{2,1,0:T(8,128)} %bitcast.3), calls=%async_computation.1 | async-start | bytes 1310720 | tf_op jit(solution)/shard_map/all_to_all | solution.py:322
  45.1 8.2 %collective-permute-start.2 = (f32[512,128]{1,0:T(8,128)S(1)}, f32[512,128]{1,0:T(8,128)S(1)}, u32[]{:S(2)}, u32[]{:S(2)}) collective-permute-start(f32[512,128]{1,0:T(8,128)S(1)} %get-tuple-element.27), channel_id=1, source_target_pairs={{0,16},{2,18},{4,20},{6,22},{8,24},{10,26},{12,28},{14,30},{16,0},... | collective-permute-start | bytes 786440 | tf_op jit(solution)/shard_map/ppermute | solution.py:319
